TPU v7x, 32 devices: a whole 2x2x4 slice. The times are simulated.
32 devices in a mesh: dp: 8 (over z, y), tensor: 4 (over x, core).
Axes of the slice: x: 2, y: 2, z: 4, core: 2. Of those that a mesh axis runs over, the one named last changes fastest.
Arguments:
- tokens: bfloat16 [8192, 768], P('dp'), may hold values from -6 to 6
- text_states: bfloat16 [32, 77, 768], P('dp'), may hold values from -6 to 6
- clip_len: int32 [32], P('dp'), may hold values from 0 to 1024, as said below
- text_len: int32 [32], P('dp'), may hold values from 1 to 77
- timesteps: int32 [32], P('dp'), may hold values from 0 to 999
- q_weight: bfloat16 [768, 768], P(None, 'tensor'), may hold values from -0.21875 to 0.21875
- k_weight: bfloat16 [768, 768], P(None, 'tensor'), may hold values from -0.21875 to 0.21875
- v_weight: bfloat16 [768, 768], P(None, 'tensor'), may hold values from -0.21875 to 0.21875
- o_weight: bfloat16 [768, 768], P('tensor'), may hold values from -3 to 3
- cross_q: bfloat16 [768, 768], P(None, 'tensor'), may hold values from -0.21875 to 0.21875
- cross_k: bfloat16 [768, 768], P(None, 'tensor'), may hold values from -0.21875 to 0.21875
- cross_v: bfloat16 [768, 768], P(None, 'tensor'), may hold values from -0.21875 to 0.21875
- cross_o: bfloat16 [768, 768], P('tensor'), may hold values from -1.25 to 1.25
- mlp_in: bfloat16 [768, 3072], P(None, 'tensor'), may hold values from -0.3125 to 0.3125
- mlp_out: bfloat16 [3072, 768], P('tensor'), may hold values from -0.21875 to 0.21875
- mod_weight: bfloat16 [768, 6912], P(None, 'tensor'), may hold values from -0.21875 to 0.21875
- mod_bias: bfloat16 [6912], P('tensor'), may hold values from -3 to 3
- cotangent: bfloat16 [8192, 768], P('dp'), may hold values from -6 to 6
Outputs:
- mixed: bfloat16 [8192, 768], P('dp')
- token_grad: bfloat16 [8192, 768], P('dp')
- q_weight_grad: float32 [768, 768], P(None, 'tensor')
- k_weight_grad: float32 [768, 768], P(None, 'tensor')
- v_weight_grad: float32 [768, 768], P(None, 'tensor')
- o_weight_grad: float32 [768, 768], P('tensor')
- cross_q_grad: float32 [768, 768], P(None, 'tensor')
- cross_k_grad: float32 [768, 768], P(None, 'tensor')
- cross_v_grad: float32 [768, 768], P(None, 'tensor')
- cross_o_grad: float32 [768, 768], P('tensor')
- mlp_in_grad: float32 [768, 3072], P(None, 'tensor')
- mlp_out_grad: float32 [3072, 768], P('tensor')
- mod_weight_grad: float32 [768, 6912], P(None, 'tensor')
- mod_bias_grad: float32 [6912], P('tensor')
Inputs may be any that keep to these rules, and one draw needn't show every extreme that they name: `clip_len`: each aligned run of 4 entries lists, in order, clip lengths of 256, 512 or 1024 frames that sum to 1024, followed by zeros for unused slots.
All inputs are finite; a program needn't handle non-finite values.
Results may differ from a plain program's by a relative error of at most 0.028.
Values may be sent and summed in bfloat16 or wider, within the bound.
No kernel may reach another device: no remote copies, remote signals or barrier semaphores. Data moves between devices by JAX's collectives and lax.ppermute only.
A program may use at most 192 MiB of HBM per device.

v0:
```python
import functools
import math

import jax
import jax.numpy as jnp
from jax import lax
from jax.experimental import pallas as pl
from jax.experimental.pallas import tpu as pltpu
from jax.sharding import PartitionSpec as P

HEAD = 64
BLOCK = 256
EPSILON = 1e-06
MASKED = -1000000000.0
CURVE = math.sqrt(2.0 / math.pi)
CUBIC = 0.044715
F32 = jnp.float32
BF16 = jnp.bfloat16


def dot_nn(a, b):
    return lax.dot_general(a, b, (((1,), (0,)), ((), ())), preferred_element_type=F32)


def dot_nt(a, b):
    return lax.dot_general(a, b, (((1,), (1,)), ((), ())), preferred_element_type=F32)


def dot_tn(a, b):
    return lax.dot_general(a, b, (((0,), (0,)), ((), ())), preferred_element_type=F32)


def normalize(values):
    centered = values - jnp.mean(values, axis=-1, keepdims=True)
    inverse = lax.rsqrt(jnp.mean(centered * centered, axis=-1, keepdims=True) + EPSILON)
    return centered * inverse, inverse


def norm_back(grad, normed, inverse):
    first = jnp.mean(grad, axis=-1, keepdims=True)
    second = jnp.mean(grad * normed, axis=-1, keepdims=True)
    return inverse * (grad - first - normed * second)


def column_sum(values):
    return jnp.sum(values, axis=0, keepdims=True)


def three_parts(column):
    high = column.astype(BF16).astype(F32)
    rest = column - high
    middle = rest.astype(BF16).astype(F32)
    return high, middle, rest - middle


def head_slice(rows, head):
    piece = rows[:, head * HEAD : (head + 1) * HEAD]
    return jnp.concatenate([piece, jnp.zeros_like(piece)], axis=1)


class View:
    def __init__(self, ref):
        self.view = ref

    def ref(self):
        return self.view


class Place:
    def __init__(self, ref):
        self.ref = ref

    def __getitem__(self, index):
        return self.ref[0, index]


def run(kernel, outs, scalars, arrays, late=(), scratch=(), cost=0.001, vmem=10):
    in_vmem = pl.BlockSpec(memory_space=pltpu.VMEM)
    pairs = [entry if isinstance(entry, tuple) else (entry, None) for entry in late]
    n_plain = len(arrays)

    def wrapped(place, *refs):
        place = Place(place)
        views = []
        for ref, (_, block) in zip(refs[n_plain:], pairs):
            views.append(View(ref if block is None else ref.at[token_rows(block(place)), :]))
        kernel(place, *refs[:n_plain], *views, *refs[n_plain + len(pairs) :])

    return pl.pallas_call(
        wrapped,
        name=getattr(kernel, "__name__", "advance"),
        out_shape=[jax.ShapeDtypeStruct(shape, kind) for shape, kind in outs],
        in_specs=[in_vmem] * (1 + n_plain + len(pairs)),
        out_specs=[in_vmem] * len(outs),
        scratch_shapes=[pltpu.VMEM(shape, kind) for shape, kind in scratch],
        compiler_params=pltpu.CompilerParams(vmem_limit_bytes=vmem * 1024 * 1024),
        cost_estimate=pl.CostEstimate(flops=int(cost * 1_000_000_000), bytes_accessed=1000, transcendentals=0),
    )(scalars, *arrays, *[array for array, _ in pairs])


SLOT, CORE, ROW, END, TENSOR, OWN, FAR, LIMIT = 0, 4, 5, 6, 7, 8, 10, 12
ORDER = (0, 2, 1, 3)


def block_of(place, chunk):
    return place[CORE] * 2 + chunk


def mod_row(mod, slot, component, model):
    return mod[pl.ds(slot, 1), component * model : (component + 1) * model]


def quad_cols(quad):
    if isinstance(quad, int):
        return slice(quad * 4 * HEAD, (quad + 1) * 4 * HEAD)
    return pl.ds(pl.multiple_of(quad * 4 * HEAD, 4 * HEAD), 4 * HEAD)


def token_rows(block):
    return pl.ds(pl.multiple_of(block * BLOCK, BLOCK), BLOCK)


def text_kernel(place, text, weights, packed):
    rows = text.shape[1]
    wide = weights.shape[0]
    for slot in range(text.shape[0]):
        first = rows * (slot % 2)
        left = wide * (slot // 2)
        packed[first : first + rows, left : left + wide] = dot_nt(text[slot], weights[...]).astype(BF16)


def unpack_kernel(place, q0, o0, q1, o1, part2, rest2, part3, rest3, t0, t1, t2, t3, cqt, co, kall, vall):
    width = q0.shape[0]
    half = width // 2
    rows = kall.shape[1]
    for index, (query, out) in enumerate(((q0, o0), (q1, o1))):
        cqt[index * width : (index + 1) * width, :] = query[...]
        co[index * width : (index + 1) * width, :] = out[...]
    for index, (part, rest) in enumerate(((part2, rest2), (part3, rest3))):
        for piece, row in ((part, place[ROW]), (rest, 1 - place[ROW])):
            at = pl.ds(pl.multiple_of((index + 2) * width + row * half, half), half)
            cqt[at, :] = piece[:half, :]
            co[at, :] = piece[half:, :]
    for slot in range(kall.shape[0]):
        first = rows * (slot % 2)
        left = 2 * width * (slot // 2)
        both = [t[first : first + rows, left : left + 2 * width] for t in (t0, t1, t2, t3)]
        kall[slot] = jnp.concatenate([b[:, :width] for b in both], axis=1)
        vall[slot] = jnp.concatenate([b[:, width:] for b in both], axis=1)


def attend_chunk(place, chunk, qa_in, ka, va, wo, part_own, part_send, qa_out, att):
    heads = ka.shape[0]
    lane = lax.broadcasted_iota(jnp.int32, (BLOCK, 2 * HEAD), 1)
    spot = (lane >= HEAD + 4) & (lane < HEAD + 7)

    @pl.loop(0, 2)
    def _(side):
        at = token_rows(2 * chunk + side)
        here = token_rows(side)
        pieces = []
        for head in range(heads):
            queries = qa_in[head, at, :]
            scores = dot_nt(queries, ka[head])
            top = jnp.max(scores, axis=1, keepdims=True)
            raised = jnp.exp(scores - top).astype(BF16)
            out = dot_nn(raised, va[head])
            total = out[:, HEAD : HEAD + 1]
            pieces.append(out[:, :HEAD] * (1.0 / total))
            high, middle, low = three_parts(-(top + jnp.log(total)))
            more = jnp.where(lane == HEAD + 4, high, jnp.where(lane == HEAD + 5, middle, low))
            qa_out[head, here, :] = jnp.where(spot, more, queries.astype(F32)).astype(BF16)
        attended = jnp.concatenate(pieces, axis=1).astype(BF16)
        att[here, :] = attended
        out = dot_nn(attended, wo[...]).astype(BF16)

        @pl.when(place[CORE] == side)
        def _():
            part_own[...] = out

        @pl.when(place[CORE] != side)
        def _():
            part_send[...] = out


def self_first(place, mod, weights, tokens, wo, part_own, part_send, qa, ka, va, qa_out, att, h1):
    model = mod.shape[1] // 9
    lane = lax.broadcasted_iota(jnp.int32, (BLOCK, 2 * HEAD), 1)
    keep = lane < HEAD
    width = weights.shape[0] // 3
    tokens = tokens.ref()
    slots = [place[SLOT + block] for block in ORDER]

    @pl.loop(0, len(ORDER))
    def _(position):
        rows = token_rows(position)
        first = jnp.where(position == 0, slots[0], slots[1])
        slot = jnp.where(position < 2, first, jnp.where(position == 2, slots[2], slots[3]))
        block = lax.rem(position, 2) * 2 + lax.div(position, 2)
        normed, _ = normalize(tokens[token_rows(block), :].astype(F32))
        hidden = (normed * (1.0 + mod_row(mod, slot, 1, model)) + mod_row(mod, slot, 0, model)).astype(BF16)
        h1[rows, :] = hidden
        rows_qkv = dot_nt(hidden, weights[...])
        q = rows_qkv[:, :width].astype(BF16).astype(F32) * (HEAD**-0.5)
        k = rows_qkv[:, width : 2 * width]
        v = rows_qkv[:, 2 * width :]
        mine = lane == HEAD + slot
        q_more = jnp.where(mine, 1.0, 0.0)
        k_more = jnp.where((lane >= HEAD + 4) & (lane < HEAD + 7), 1.0, 0.0)
        k_more = jnp.where((lane >= HEAD) & (lane < HEAD + 4) & jnp.logical_not(mine), MASKED, k_more)
        v_more = jnp.where((lane >= HEAD) & (lane < HEAD + 3), 1.0, 0.0)
        for head in range(ka.shape[0]):
            qa[head, rows, :] = jnp.where(keep, head_slice(q, head), q_more).astype(BF16)
            ka[head, rows, :] = jnp.where(keep, head_slice(k, head), k_more).astype(BF16)
            va[head, rows, :] = jnp.where(keep, head_slice(v, head), v_more).astype(BF16)
    attend_chunk(place, 0, qa, ka, va, wo.ref(), part_own, part_send, qa_out, att)


def self_second(place, qa, ka, va, wo, part_own, part_send, qa_out, att):
    attend_chunk(place, 1, qa, ka, va, wo.ref(), part_own, part_send, qa_out, att)


def quad_stack(rows, masks):
    return jnp.concatenate([rows * mask for mask in masks], axis=0)


def quad_masks():
    lane = lax.broadcasted_iota(jnp.int32, (1, 4 * HEAD), 1)
    return [jnp.where((lane >= u * HEAD) & (lane < (u + 1) * HEAD), 1.0, 0.0) for u in range(4)]


def quad_probs(scores, limit, text_rows):
    key_row = lax.broadcasted_iota(jnp.int32, (text_rows, 1), 0)
    bias = jnp.where(key_row < limit, 0.0, MASKED)
    probs = []
    for u in range(4):
        part = scores[u * text_rows : (u + 1) * text_rows, :] + bias
        raised = jnp.exp(part - jnp.max(part, axis=0, keepdims=True))
        probs.append(raised * (1.0 / jnp.sum(raised, axis=0, keepdims=True)))
    return probs


def middle_chunk(
    place, chunk, mod, sum_own, sum_far, cqt, co, kall, vall, tokens, cot, win0, wout0, win1, wout1, x2_before,
    h3g_out, h3_out, act0, act1, pg0, pg1, b3g_out, x1_out, b2_out, h2_out, q2_out, cr_out, b3_out, x2_out,
):
    model = cqt.shape[1]
    text_rows = kall.shape[1]
    slot = place[OWN + chunk]

    def m(component):
        return mod_row(mod, slot, component, model)

    x1 = tokens.ref()[...].astype(F32) + m(2) * (sum_own[...].astype(F32) + sum_far[...].astype(F32))
    x1_out[...] = x1
    normed, _ = normalize(x1)
    h2 = (normed * (1.0 + m(4)) + m(3)).astype(BF16)
    h2_out[...] = h2
    q2 = (dot_nt(h2, cqt[...]).astype(BF16).astype(F32) * (HEAD**-0.5)).astype(BF16)
    q2_out[...] = q2
    masks = [mask.astype(BF16) for mask in quad_masks()]
    limit = place[LIMIT + chunk]


    def by_quad(quad):
        cols = quad_cols(quad)
        scores = dot_nt(quad_stack(kall[slot, :, cols], masks), q2_out[:, cols])
        probs = jnp.concatenate(quad_probs(scores, limit, text_rows), axis=0)
        cr_out[:, cols] = dot_tn(probs.astype(BF16), quad_stack(vall[slot, :, cols], masks)).astype(BF16)

    if chunk == 1:
        pl.loop(0, model // (4 * HEAD))(by_quad)
    else:
        for quad in range(model // (4 * HEAD)):
            by_quad(quad)
    b2 = dot_nn(cr_out[...], co[...])
    b2_out[...] = b2
    x2 = x1 + m(5) * b2
    x2_out[chunk * BLOCK : (chunk + 1) * BLOCK, :] = x2
    normed, _ = normalize(x2)
    h3 = (normed * (1.0 + m(7)) + m(6)).astype(BF16)
    h3_out[...] = h3
    b3g = (cot.ref()[...].astype(F32) * m(8)).astype(BF16)
    b3g_out[...] = b3g
    b3 = h3g = None
    for win, wout, act_out, pg_out in ((win0, wout0, act0, pg0), (win1, wout1, act1, pg1)):
        win, wout = win.ref(), wout.ref()
        pre = dot_nn(h3, win[...])
        square = pre * pre
        bent = jnp.tanh(CURVE * (pre + CUBIC * (square * pre)))
        act = (0.5 * pre * (1.0 + bent)).astype(BF16)
        act_out[...] = act
        slope = 0.5 * (1.0 + bent) + 0.5 * pre * (1.0 - bent * bent) * (CURVE * (1.0 + 3.0 * CUBIC * square))
        b3_half = dot_nn(act, wout[...])
        pg = (dot_nt(b3g, wout[...]) * slope).astype(BF16)
        pg_out[...] = pg
        h3g_half = dot_nt(pg, win[...])
        b3 = b3_half if b3 is None else b3 + b3_half
        h3g = h3g_half if h3g is None else h3g + h3g_half
    b3_out[...] = b3.astype(BF16)
    if chunk:
        x2_out[0:BLOCK, :] = x2_before.ref()[...]
    h3g_out[...] = h3g.astype(BF16)


def middle_first(place, *refs):
    middle_chunk(place, 0, *refs[:13], None, *refs[13:])


def middle_second(place, *refs):
    middle_chunk(place, 1, *refs)


def stacked(first, second):
    return jnp.concatenate([first[...], second[...]], axis=0)


def mlp_back(
    place, h3a, h3b, pg0a, pg0b, pg1a, pg1b, act0a, act0b, act1a, act1b, b3ga, b3gb,
    in_own, in_send, out_own, out_send,
):
    half = in_own.shape[1]
    grads = (stacked(pg0a, pg0b), stacked(pg1a, pg1b))
    for part in range(2):
        cols = slice(part * half, (part + 1) * half)
        rows = jnp.concatenate([h3a[:, cols], h3b[:, cols]], axis=0)
        for out, grad in ((in_send, grads[1]), (in_own, grads[0])):
            out[part ^ place[ROW]] = dot_tn(rows, grad).astype(BF16)
    grad = stacked(b3ga, b3gb)
    for out, first, second in ((out_send, act1a, act1b), (out_own, act0a, act0b)):
        for part in range(2):
            cols = slice(part * half, (part + 1) * half)
            rows = jnp.concatenate([first[:, cols], second[:, cols]], axis=0)
            out[part ^ place[ROW]] = dot_tn(rows, grad).astype(BF16)


def cross_chunk(
    place, chunk, mod, h3g_own, h3g_far, kall, vall, cqt, co, x1_in, b2_in, cot, q2_in, sum_own, sum_far,
    b1g_out, dq_out, b2g_out, dk_out, dv_out, sums, x1g_out, out_grad,
):
    model = cqt.shape[1]
    text_rows = kall.shape[1]
    slot = place[OWN + chunk]

    def m(component):
        return mod_row(mod, slot, component, model)

    x1 = x1_in.ref()[...]
    b2 = b2_in.ref()[...]
    h3g = h3g_own[...].astype(F32) + h3g_far[...].astype(F32)
    normed, inverse = normalize(x1 + m(5) * b2)
    sums[4:5, :] = column_sum(h3g)
    sums[5:6, :] = column_sum(h3g * normed)
    x2g = cot.ref()[...].astype(F32) + norm_back(h3g * (1.0 + m(7)), normed, inverse)
    sums[3:4, :] = column_sum(x2g * b2)
    b2g = (x2g * m(5)).astype(BF16)
    b2g_out[...] = b2g
    out_grad[...] = dot_nt(b2g, co[...]).astype(BF16)
    masks = quad_masks()
    low = [mask.astype(BF16) for mask in masks]
    limit = place[LIMIT + chunk]

    def by_quad(quad):
        cols = quad_cols(quad)
        queries = q2_in.ref()[:, cols]
        grads = out_grad[:, cols]
        keys = quad_stack(kall[slot, :, cols], low)
        values = quad_stack(vall[slot, :, cols], low)
        probs = quad_probs(dot_nt(keys, queries), limit, text_rows)
        prob_grad = dot_nt(values, grads)
        score_grad = []
        for u in range(4):
            part = prob_grad[u * text_rows : (u + 1) * text_rows, :]
            row_dot = jnp.sum(probs[u] * part, axis=0, keepdims=True)
            score_grad.append((probs[u] * (part - row_dot)).astype(BF16))
        score_grad = jnp.concatenate(score_grad, axis=0)
        dv = dot_nn(jnp.concatenate(probs, axis=0).astype(BF16), grads)
        dk = dot_nn(score_grad, queries)
        dq_out[:, cols] = (dot_tn(score_grad, keys) * (HEAD**-0.5)).astype(BF16)
        for wide, out in ((dk, dk_out), (dv, dv_out)):
            total = None
            for u in range(4):
                part = wide[u * text_rows : (u + 1) * text_rows, :] * masks[u]
                total = part if total is None else total + part
            out[:, cols] = total.astype(BF16)
    if chunk:
        for quad in range(model // (4 * HEAD)):
            by_quad(quad)
    else:
        pl.loop(0, model // (4 * HEAD))(by_quad)
    h2g = dot_nn(dq_out[...], cqt[...])
    normed, inverse = normalize(x1)
    sums[1:2, :] = column_sum(h2g)
    sums[2:3, :] = column_sum(h2g * normed)
    x1g = x2g + norm_back(h2g * (1.0 + m(4)), normed, inverse)
    x1g_out[...] = x1g
    branch = sum_own.ref()[...].astype(F32) + sum_far.ref()[...].astype(F32)
    sums[0:1, :] = column_sum(x1g * branch)
    sums[6:8, :] = jnp.zeros((2, model), F32)
    b1g_out[...] = (x1g * m(2)).astype(BF16)


def cross_first(place, *refs):
    cross_chunk(place, 0, *refs)


def cross_second(place, *refs):
    cross_chunk(place, 1, *refs)


def cross_weights(
    place, dqa, dqb, b2ga, b2gb, dka, dkb, dva, dvb, h2a, h2b, cra, crb, text, own, send,
):
    width = own.shape[1] // 2
    row = place[ROW]
    h2a, h2b, cra, crb, text = h2a.ref(), h2b.ref(), cra.ref(), crb.ref(), text.ref()
    slots = [place[OWN + chunk] for chunk in range(2)]

    @pl.loop(0, h2a.shape[1] // BLOCK)
    def _(part):
        to = token_rows(part)
        hidden = jnp.concatenate([h2a[:, to], h2b[:, to]], axis=0)
        grads = jnp.concatenate([b2ga[:, to], b2gb[:, to]], axis=0)
        texts = [text[slot, :, to] for slot in slots]
        for member, out in ((1, send), (0, own)):
            start = (member * width // 128) * 128
            skip = member * width - start
            cols = slice(start, start + 2 * 128)
            kept = slice(skip, skip + width)

            def two(first, second):
                return jnp.concatenate([first[:, cols], second[:, cols]], axis=0)

            top, bottom = slice(0, width), slice(width, 2 * width)
            out[row, top, to] = dot_tn(two(dqa, dqb), hidden)[kept].astype(BF16)
            out[row, bottom, to] = (dot_tn(dka[:, cols], texts[0]) + dot_tn(dkb[:, cols], texts[1]))[kept].astype(BF16)
            out[1 - row, top, to] = (dot_tn(dva[:, cols], texts[0]) + dot_tn(dvb[:, cols], texts[1]))[kept].astype(
                BF16
            )
            out[1 - row, bottom, to] = dot_tn(two(cra, crb), grads)[kept].astype(BF16)


def keys_back(block, qa, ka, va, da, dq_sum):
    rows = token_rows(block)
    dks = []
    dvs = []
    for head in range(ka.shape[0]):
        keys = ka[head, rows, :]
        probs = jnp.exp(dot_nt(keys, qa[head]))
        prob_grad = dot_nt(va[head, rows, :], da[head])
        score_grad = (probs * prob_grad).astype(BF16)
        dvs.append(dot_nn(probs.astype(BF16), da[head])[:, :HEAD])
        dks.append(dot_nn(score_grad, qa[head])[:, :HEAD])
        dq = dot_tn(score_grad, keys)
        dq_sum[head] += dq
    return jnp.concatenate(dks, axis=1).astype(BF16), jnp.concatenate(dvs, axis=1).astype(BF16)


def self_back_first(
    place, b1g_a, b1g_b, far_a, far_b, wo, att_a, att_b, qa_a, qa_b, ka, va,
    b1g, att, qa, da, dq_sum, dk_all, dv_all,
):
    blocks = b1g.shape[0] // BLOCK
    heads = da.shape[0]
    core = place[CORE]
    for chunk, (own, far) in enumerate(((b1g_a, far_a), (b1g_b, far_b))):
        b1g[token_rows(2 * chunk + core), :] = own[...]
        b1g[token_rows(2 * chunk + 1 - core), :] = far[...]
    wo = wo.ref()
    att[0 : 2 * BLOCK, :] = att_a.ref()[...]
    att[2 * BLOCK : 4 * BLOCK, :] = att_b.ref()[...]
    lane = lax.broadcasted_iota(jnp.int32, (BLOCK, 2 * HEAD), 1)

    @pl.loop(0, blocks)
    def _(block):
        rows = token_rows(block)
        grads = dot_nt(b1g[rows, :], wo[...]).astype(BF16).astype(F32)
        dots = grads * att[rows, :].astype(F32)
        for head in range(heads):
            row_dot = jnp.sum(dots[:, head * HEAD : (head + 1) * HEAD], axis=1, keepdims=True)
            high, middle, low = three_parts(-row_dot)
            more = jnp.where(lane == HEAD, high, jnp.where(lane == HEAD + 1, middle, low))
            more = jnp.where(lane < HEAD + 3, more, 0.0)
            da[head, rows, :] = jnp.where(lane < HEAD, head_slice(grads, head), more).astype(BF16)
    qa[:, 0 : 2 * BLOCK, :] = qa_a.ref()[...]
    qa[:, 2 * BLOCK : 4 * BLOCK, :] = qa_b.ref()[...]
    ka, va = ka.ref(), va.ref()
    dq_sum[...] = jnp.zeros_like(dq_sum)

    @pl.loop(0, 2)
    def _(block):
        rows = token_rows(block)
        dk_all[rows, :], dv_all[rows, :] = keys_back(block, qa, ka, va, da, dq_sum)


def self_back_second(
    place, b1g, att, qa, da, dq_in, dk_in, dv_in, weights, ka, va, h1,
    part_own, part_send, dw_keep, dw_give,
    dq_sum, grad_all,
):
    blocks = b1g.shape[0] // BLOCK
    heads = da.shape[0]
    core = place[CORE]
    width = heads * HEAD
    ka, va = ka.ref(), va.ref()
    dq_sum[...] = dq_in[...]
    grad_all[0 : 2 * BLOCK, width : 2 * width] = dk_in[0 : 2 * BLOCK, :]
    grad_all[0 : 2 * BLOCK, 2 * width : 3 * width] = dv_in[0 : 2 * BLOCK, :]

    @pl.loop(2, blocks)
    def _(block):
        rows = token_rows(block)
        dk, dv = keys_back(block, qa, ka, va, da, dq_sum)
        grad_all[rows, width : 2 * width] = dk
        grad_all[rows, 2 * width : 3 * width] = dv
    h1 = h1.ref()

    @pl.loop(0, blocks)
    def _(block):
        rows = token_rows(block)
        dq = jnp.concatenate([dq_sum[head, rows, :HEAD] for head in range(heads)], axis=1)
        grad_all[rows, 0:width] = (dq * (HEAD**-0.5)).astype(BF16)
        out = dot_nn(grad_all[rows, :], weights[...]).astype(BF16)
        side = lax.rem(block, 2)
        out_rows = token_rows(lax.div(block, 2))

        @pl.when(core == side)
        def _():
            part_own[out_rows, :] = out

        @pl.when(core != side)
        def _():
            part_send[out_rows, :] = out

    @pl.loop(0, h1.shape[1] // BLOCK)
    def _(part):
        cols = token_rows(part)
        grads = dot_tn(grad_all[...], h1[:, cols]).astype(BF16)
        query_key = (grads[:width], grads[width : 2 * width])
        value_out = (grads[2 * width :], dot_tn(att[...], b1g[:, cols]).astype(BF16))
        for flag, first, second in ((0, query_key, value_out), (1, value_out, query_key)):

            @pl.when(place[ROW] == flag)
            def _():
                for index in range(2):
                    rows = slice(index * width, (index + 1) * width)
                    dw_keep[rows, cols] = first[index]
                    dw_give[rows, cols] = second[index]


def mixed_kernel(place, mod, b3a, b3b, far_a, far_b, x2, cot_a, cot_b, mixed_a, mixed_b, sums):
    model = mixed_a.shape[1]
    for chunk, (own, far, cot) in enumerate(((b3a, far_a, cot_a), (b3b, far_b, cot_b))):
        mixed = (mixed_a, mixed_b)[chunk]
        rows = slice(chunk * BLOCK, (chunk + 1) * BLOCK)
        slot = place[OWN + chunk]
        b3 = own[...].astype(F32) + far[...].astype(F32)
        mixed[...] = (x2[rows, :] + mod_row(mod, slot, 8, model) * b3).astype(BF16)
        sums[chunk] = column_sum(cot.ref()[...].astype(F32) * b3)


def final_kernel(
    place, mod, h1g_own, h1g_far, sums_a, sums_b, sums_mixed, tokens_a, tokens_b, x1ga, x1gb, grad_a, grad_b, slot_sums,
):
    model = grad_a.shape[1]
    slot_sums[...] = jnp.zeros_like(slot_sums)
    for chunk, (x1g, sums, tokens) in enumerate(((x1ga, sums_a, tokens_a), (x1gb, sums_b, tokens_b))):
        rows = slice(chunk * BLOCK, (chunk + 1) * BLOCK)
        slot = place[OWN + chunk]
        h1g = h1g_own[rows, :].astype(F32) + h1g_far[rows, :].astype(F32)
        normed, inverse = normalize(tokens.ref()[...].astype(F32))
        scaled = h1g * (1.0 + mod_row(mod, slot, 1, model))
        (grad_a, grad_b)[chunk][...] = (x1g.ref()[...] + norm_back(scaled, normed, inverse)).astype(BF16)
        terms = [column_sum(h1g), column_sum(h1g * normed)]
        terms += [sums[i : i + 1, :] for i in range(6)] + [sums_mixed[chunk]]
        for component, term in enumerate(terms):
            slot_sums[pl.ds(slot, 1), component * model : (component + 1) * model] += term


def join_cores(place, mine_a, mine_b, other_a, other_b, out):
    for chunk, (mine, other) in enumerate(((mine_a, other_a), (mine_b, other_b))):
        out[token_rows(place[CORE] * 2 + chunk), :] = mine[...]
        out[token_rows((1 - place[CORE]) * 2 + chunk), :] = other[...]


def join_rows(place, mine, other, out):
    count = mine.shape[0]
    out[pl.ds(pl.multiple_of(place[ROW] * count, BLOCK // 2), count), :] = mine[...].astype(F32)
    out[pl.ds(pl.multiple_of((1 - place[ROW]) * count, BLOCK // 2), count), :] = other[...].astype(F32)


def join_four(place, mine, other, first, second, third, fourth):
    width = first.shape[0]
    for flag, top, bottom in ((0, mine, other), (1, other, mine)):

        @pl.when(place[ROW] == flag)
        def _():
            first[...] = top[:width, :].astype(F32)
            second[...] = top[width:, :].astype(F32)
            third[...] = bottom[:width, :].astype(F32)
            fourth[...] = bottom[width:, :].astype(F32)


def slot_kernel(place, own, far, silu, out):
    model = silu.shape[1]
    count = out.shape[1] - model
    out[:, :model] = silu[...].astype(F32)
    for index in range(own.shape[1] // count):
        cols = slice(index * count, (index + 1) * count)

        @pl.when(place[TENSOR] == index)
        def _():
            out[:, model:] = (own[:, cols] + far[:, cols]).astype(BF16).astype(F32)


def advance_kernel(roles, place, *refs):
    refs = list(refs)
    values, got = {}, {}
    for role in roles:
        values[role] = refs.pop(0)
    for name in ("row", "column", "middle"):
        if any(role in roles for role in {"row": "a", "column": "bd", "middle": "c"}[name]):
            got[name] = refs.pop(0)
    outs = {role: refs.pop(0) for role in roles}
    end = place[END]
    if "a" in roles:
        outs["a"][...] = added(values["a"][...], got["row"][...])
    if "c" in roles:

        @pl.when(end == 0)
        def _():
            outs["c"][...] = added(values["c"][...], got["middle"][...])

        @pl.when(end != 0)
        def _():
            outs["c"][...] = values["c"][...]

    if "b" in roles:

        @pl.when(end == 0)
        def _():
            outs["b"][...] = added(values["b"][...], got["column"][...])

        @pl.when(end != 0)
        def _():
            outs["b"][...] = values["b"][...]

    if "d" in roles:

        @pl.when(end == 0)
        def _():
            outs["d"][...] = values["d"][...]

        @pl.when(end != 0)
        def _():
            outs["d"][...] = got["column"][...]

    if refs:

        @pl.when(end == 0)
        def _():
            refs[0][...] = outs["c"][...]

        @pl.when(end != 0)
        def _():
            refs[0][...] = outs["a"][...]


def added(first, second):
    return (first.astype(F32) + second.astype(F32)).astype(BF16)


def solution(mesh):
    n_dp = mesh.shape["dp"]
    n_tensor = mesh.shape["tensor"]
    n_col = n_dp // 2
    dp_bits = int(math.log2(n_dp))

    def tensor_swap(value, flip):
        return lax.ppermute(value, "tensor", [(i, i ^ flip) for i in range(n_tensor)])

    def core_swap(value):
        return tensor_swap(value, 1)

    def far_swap(value):
        return tensor_swap(value, 2)

    def dp_swap(value, flip):
        return lax.ppermute(value, "dp", [(i, i ^ flip) for i in range(n_dp)])

    def tie(*values):
        return lax.optimization_barrier(values) if values else ()

    def pair_up(flag, mine, other):
        return jnp.concatenate([jnp.where(flag == 0, mine, other), jnp.where(flag == 0, other, mine)], axis=0)

    def local(
        tokens, text_states, clip_len, text_len, timesteps, q_weight, k_weight, v_weight, o_weight,
        cross_q, cross_k, cross_v, cross_o, mlp_in, mlp_out, mod_weight, mod_bias, cotangent,
    ):
        count, model = tokens.shape
        slots, text_rows = text_states.shape[:2]
        width = o_weight.shape[0]
        heads = width // HEAD
        half = count // 2
        text_pad = -(-text_rows // 16) * 16
        tensor_at = lax.axis_index("tensor")
        dp_at = lax.axis_index("dp")
        core = tensor_at & 1
        row = dp_at & 1
        column = dp_at >> 1

        ends = jnp.cumsum(clip_len)
        starts = jnp.arange(count // BLOCK, dtype=jnp.int32) * BLOCK
        slot_of = jnp.sum((starts[:, None] >= ends[None, :]).astype(jnp.int32), axis=1)
        end = (column == 0) | (column == n_col - 1)
        own_slots = lax.dynamic_slice_in_dim(slot_of, core * 2, 2, 0)
        far_slots = lax.dynamic_slice_in_dim(slot_of, (1 - core) * 2, 2, 0)
        limits = jnp.sum(jnp.where(own_slots[:, None] == jnp.arange(slots)[None, :], text_len[None, :], 0), axis=1)
        single = jnp.stack([core, row, end.astype(jnp.int32), tensor_at])
        place = jnp.concatenate([slot_of, single, own_slots, far_slots, limits])
        place = jnp.pad(place[None, :], ((0, 7), (0, 128 - place.shape[0])))
        place = place.astype(jnp.int32)

        query_own = cross_q.T
        part_own = jnp.concatenate(
            [lax.dynamic_slice_in_dim(w, row * (width // 2), width // 2, 0) for w in (query_own, cross_o)], axis=0
        )
        text_weights = jnp.concatenate([cross_k.T, cross_v.T], axis=0)
        text = jnp.pad(text_states, ((0, 0), (0, text_pad - text_rows), (0, 0)))
        self_weights = jnp.concatenate([q_weight.T, k_weight.T, v_weight.T], axis=0)

        half_width = model // 2
        ramp = jnp.arange(half_width).astype(F32)
        frequency = jnp.exp(ramp * (-math.log(10000.0) / half_width))
        angles = timesteps.astype(F32)[:, None] * frequency[None, :]
        embed = jnp.concatenate([jnp.cos(angles), jnp.sin(angles)], axis=1)
        silu_low = jax.nn.silu(embed).astype(BF16)
        part_far = far_swap(part_own)
        wout1 = core_swap(mlp_out)
        mod_own = dot_nn(silu_low, mod_weight) + mod_bias.astype(F32)
        mod_far = [tensor_swap(mod_own, flip) for flip in range(1, n_tensor)]
        (text_own,) = run(text_kernel, [((2 * text_pad, model), BF16)], place, [text, text_weights], cost=1.0)
        text_own, self_weights, wout1, *mod_far = tie(text_own, self_weights, wout1, *mod_far)
        text_far = far_swap(text_own)
        query_own, out_own, text_own = tie(query_own, cross_o, text_own)
        query1, out1, text1 = core_swap(query_own), core_swap(out_own), core_swap(text_own)
        mod_all = jnp.stack([mod_own] + mod_far)
        mod = jnp.concatenate(
            [lax.dynamic_index_in_dim(mod_all, tensor_at ^ j, 0, keepdims=False) for j in range(n_tensor)], axis=1
        )

        wide = (heads, count, 2 * HEAD)
        block_wide = (heads, 2 * BLOCK, 2 * HEAD)
        one = ((BLOCK, model), BF16)
        one_f32 = ((BLOCK, model), F32)
        attend_far = [(block_wide, BF16), ((2 * BLOCK, width), BF16)]
        own_a, send_a, qa, ka, va, qa_a, att_a, h1 = run(
            self_first, [one, one] + [(wide, BF16)] * 3 + attend_far + [((count, model), BF16)], place, [mod, self_weights], cost=0.001,
            late=[tokens, o_weight],
        )
        send_a, part_far, text_far, query1, out1, text1 = tie(send_a, part_far, text_far, query1, out1, text1)
        sum_a = added(own_a, core_swap(send_a))
        sum_a, qa, part_far, text_far, win0 = tie(sum_a, qa, part_far, text_far, mlp_in)
        far_a = far_swap(sum_a)
        rest_far = dp_swap(part_far, 1)
        part3, text3, win1 = core_swap(part_far), core_swap(text_far), core_swap(win0)
        own_b, send_b, qa_b, att_b = run(
            self_second, [one, one] + attend_far, place, [qa, ka, va], late=[o_weight]
        )
        (far_a,) = tie(far_a)
        send_b, far_a, rest_far, part3, text3, win1 = tie(send_b, far_a, rest_far, part3, text3, win1)
        rest3 = core_swap(rest_far)
        sum_b = added(own_b, core_swap(send_b))
        sum_b, rest3 = tie(sum_b, rest3)
        far_b = far_swap(sum_b)
        cqt, co, kall, vall = run(
            unpack_kernel, [((model, model), BF16)] * 2 + [((slots, text_pad, model), BF16)] * 2,
            place,
            [query_own, out_own, query1, out1, part_far, rest_far, part3, rest3, text_own, text1, text_far, text3],
            cost=0.001,
        )
        shared = [cqt, co, kall, vall]

        def chunk_rows(array, chunk):
            return (array, functools.partial(block_of, chunk=chunk))

        def middle(kernel, chunk, own, far, *before):
            return run(
                kernel, [one] * 7 + [one_f32, one_f32] + [one] * 4 + [(((chunk + 1) * BLOCK, model), F32)], place,
                [mod, own, far] + shared, cost=7.5,
                late=[chunk_rows(tokens, chunk), chunk_rows(cotangent, chunk), mlp_in, mlp_out, win1, wout1, *before],
            )

        h3ga, h3a, act0a, act1a, pg0a, pg1a, b3ga, x1a, b2a, h2a, q2a, cra, b3a, x2a = middle(
            middle_first, 0, sum_a, far_a
        )
        h3ga, far_b = tie(h3ga, far_b)
        h3g_far_a = far_swap(h3ga)
        h3gb, h3b, act0b, act1b, pg0b, pg1b, b3gb, x1b, b2b, h2b, q2b, crb, b3b, x2 = middle(
            middle_second, 1, sum_b, far_b, x2a
        )
        h3gb, pg0b, h3g_far_a = tie(h3gb, pg0b, h3g_far_a)
        h3g_far_b = far_swap(h3gb)

        in_own, in_send, out_own, out_send = run(
            mlp_back, [((2, model // 2, model), BF16)] * 4, place,
            [h3a, h3b, pg0a, pg0b, pg1a, pg1b, act0a, act0b, act1a, act1b, b3ga, b3gb], cost=0.001,
        )

        def cross(kernel, chunk, h3g_own, h3g_far, x1, b2, own, far, q2):
            return run(
                kernel, [one] * 3 + [((text_pad, model), BF16)] * 2 + [((8, model), F32), one_f32], place,
                [mod, h3g_own, h3g_far, kall, vall, cqt, co],
                late=[x1, b2, chunk_rows(cotangent, chunk), q2, own, far], scratch=[one],
                cost=4.0 if chunk else 0.001,
            )

        b1g_a, dqa, b2ga, dka, dva, sums_a, x1ga = cross(
            cross_first, 0, h3ga, h3g_far_a, x1a, b2a, sum_a, far_a, q2a
        )
        in_send, out_send, b1g_a, h3g_far_b = tie(in_send, out_send, b1g_a, h3g_far_b)
        in_got, b1g_far_a = core_swap(in_send), core_swap(b1g_a)
        b1g_b, dqb, b2gb, dkb, dvb, sums_b, x1gb = cross(
            cross_second, 1, h3gb, h3g_far_b, x1b, b2b, sum_b, far_b, q2b
        )
        in_got, out_send, b1g_far_a, b1g_b, dqb, b3a = tie(in_got, out_send, b1g_far_a, b1g_b, dqb, b3a)
        in_keep, in_give = added(in_own[0], in_got[0]), added(in_own[1], in_got[1])

        across = [(i, i ^ 1) for i in range(n_dp)]
        neighbours = [(i, i ^ 2) for i in range(n_dp)]
        middle_pair = [(2 * a + r, 2 * b + r) for a, b in ((1, 2), (2, 1)) for r in range(2)]
        chain_rows = (model // 2, model)

        class Rounds:
            def __init__(self):
                self.values, self.column_send, self.results, self.waiting = {}, None, [], []

            def start(self, *chain):
                self.got = {}
                if n_col != 4:
                    self.waiting += [chain] if chain else []
                    return
                if chain:
                    self.values["a"] = chain[0]
                    self.got["row"] = lax.ppermute(chain[1], "dp", across)
                if "e" in self.values:
                    self.got["last"] = lax.ppermute(self.values["e"], "dp", across)
                if "b" in self.values or "d" in self.values:
                    self.got["column"] = lax.ppermute(self.column_send, "dp", neighbours)
                if "c" in self.values:
                    self.got["middle"] = lax.ppermute(self.values["c"], "dp", middle_pair)

            def finish(self, *others, early=()):
                order = [name for name in ("row", "last", "column", "middle") if name in self.got]
                settled = list(early)
                for name in order:
                    settled = list(tie(self.got[name], *settled))
                tied = tie(*settled, *others)
                self.got = dict(zip(reversed(order), tied))
                others = tied[len(order) :]
                if "last" in self.got:
                    self.results.append((self.values.pop("e"), self.got.pop("last")))
                roles = "".join(role for role in "abcd" if role in self.values)
                if not roles:
                    return others
                operands = [self.values[role] for role in roles]
                operands += [self.got[name] for name in ("row", "column", "middle") if name in self.got]
                sends = "a" in roles or "c" in roles
                both = "a" in roles and "c" in roles
                outs = run(
                    functools.partial(advance_kernel, roles), [(chain_rows, BF16)] * (len(roles) + both),
                    place, operands, cost=0.3,
                )
                done = tie(*outs, *others)
                stepped = dict(zip(roles, done))
                if sends:
                    self.column_send = done[len(roles)] if both else stepped["a" if "a" in roles else "c"]
                self.values = {{"a": "b", "b": "c", "c": "d", "d": "e"}[role]: v for role, v in stepped.items()}
                return done[len(outs) :]

            def halves(self, number):
                return self.results[number] if n_col == 4 else self.slowly(*self.waiting[number])

            def whole(self, number):
                return run(join_rows, [((model, model), F32)], place, self.halves(number))[0]

            def four(self, number):
                return run(join_four, [((width, model), F32)] * 4, place, self.halves(number))

            def slowly(self, keep, give):
                total = added(keep, lax.ppermute(give, "dp", across))
                for bit in range(1, dp_bits):
                    size, flag = total.shape[0] // 2, (dp_at >> bit) & 1
                    sent = lax.dynamic_slice_in_dim(total, (1 - flag) * size, size, 0)
                    total = added(lax.dynamic_slice_in_dim(total, flag * size, size, 0), dp_swap(sent, 1 << bit))
                for bit in reversed(range(1, dp_bits)):
                    total = pair_up((dp_at >> bit) & 1, total, dp_swap(total, 1 << bit))
                return total, lax.ppermute(total, "dp", across)

        rounds = Rounds()

        rounds.start(in_keep, in_give)
        b1g_far_b, out_got = core_swap(b1g_b), core_swap(out_send)
        out_keep, out_give = added(out_own[0], out_got[0]), added(out_own[1], out_got[1])
        b3_far_a = far_swap(b3a)
        cross_dw, cross_send = run(
            cross_weights, [((2, 2 * width, model), BF16)] * 2, place,
            [dqa, dqb, b2ga, b2gb, dka, dkb, dva, dvb], late=[h2a, h2b, cra, crb, text], cost=0.001,
        )
        b1g_far_b, cross_send = tie(b1g_far_b, cross_send)
        b1g_all, att_all, qa_all, da, dq_sum, dk_all, dv_all = run(
            self_back_first,
            [((count, model), BF16), ((count, width), BF16), (wide, BF16), (wide, BF16), (wide, F32)]
            + [((count, width), BF16)] * 2,
            place, [b1g_a, b1g_b, b1g_far_a, b1g_far_b],
            late=[o_weight, att_a, att_b, qa_a, qa_b, ka, va], cost=0.001,
        )
        b1g_all, cross_send, out_give, b3b, b3_far_a = rounds.finish(b1g_all, cross_send, out_give, b3b, b3_far_a)

        rounds.start(out_keep, out_give)
        cross_got = core_swap(cross_send)
        b3_far_b = far_swap(b3b)
        grad_own, grad_send, self_keep, self_give = run(
            self_back_second,
            [((half, model), BF16)] * 2 + [((2 * width, model), BF16)] * 2, place,
            [b1g_all, att_all, qa_all, da, dq_sum, dk_all, dv_all, self_weights], late=[ka, va, h1],
            scratch=[(wide, F32), ((count, 3 * width), BF16)],
        )
        cross_keep, cross_give = added(cross_dw[0], cross_got[0]), added(cross_dw[1], cross_got[1])
        grad_send, cross_give, self_give, b3_far_b = rounds.finish(grad_send, cross_give, self_give, b3_far_b)

        rounds.start(cross_keep, cross_give)
        h1g_own = added(grad_own, core_swap(grad_send))
        h1g_far = far_swap(h1g_own)
        mixed_a, mixed_b, sums_mixed = run(
            mixed_kernel, [one, one, ((2, 1, model), F32)],
            place, [mod, b3a, b3b, b3_far_a, b3_far_b, x2], late=[chunk_rows(cotangent, 0), chunk_rows(cotangent, 1)],
        )
        self_give, h1g_own, mixed_a, mixed_b = rounds.finish(self_give, h1g_own, mixed_a, mixed_b)

        rounds.start(self_keep, self_give)
        grad_a, grad_b, slot_sums = run(
            final_kernel, [one, one, ((slots, 9 * model), F32)],
            place, [mod, h1g_own, h1g_far, sums_a, sums_b, sums_mixed],
            late=[chunk_rows(tokens, 0), chunk_rows(tokens, 1), x1ga, x1gb],
        )
        grad_a, grad_b, slot_sums, mixed_a = rounds.finish(mixed_a, early=(grad_a, grad_b, slot_sums))

        rounds.start()
        slot_far = core_swap(slot_sums)
        mixed_far_a = core_swap(mixed_a)
        slot_far, mixed_far_a, mixed_b = rounds.finish(slot_far, mixed_far_a, mixed_b)

        rounds.start()
        (gathered,) = run(
            slot_kernel, [((slots, model + mod_weight.shape[1]), F32)], place, [slot_sums, slot_far, silu_low]
        )
        gathered = jnp.concatenate([gathered, dp_swap(gathered, 1)], axis=0)
        mixed_far_b = core_swap(mixed_b)
        gathered, mixed_far_b, grad_a, grad_b = rounds.finish(gathered, mixed_far_b, grad_a, grad_b)

        rounds.start()
        gathered = jnp.concatenate([gathered, dp_swap(gathered, 2)], axis=0)
        grad_far_a, grad_far_b = core_swap(grad_a), core_swap(grad_b)
        mlp_in_grad, mlp_out_grad = rounds.whole(0), rounds.whole(1)
        gathered, grad_far_a, grad_far_b, mlp_in_grad, mlp_out_grad = rounds.finish(
            gathered, grad_far_a, grad_far_b, mlp_in_grad, mlp_out_grad
        )

        rounds.start()
        for bit in range(2, dp_bits):
            gathered = jnp.concatenate([gathered, dp_swap(gathered, 1 << bit)], axis=0)
        (mixed,) = run(
            join_cores, [((count, model), BF16)], place, [mixed_a, mixed_b, mixed_far_a, mixed_far_b]
        )
        (token_grad,) = run(
            join_cores, [((count, model), BF16)], place, [grad_a, grad_b, grad_far_a, grad_far_b]
        )
        cross_grads = rounds.four(2)
        gathered_low = gathered.astype(BF16)
        mod_weight_grad = dot_tn(gathered_low[:, :model], gathered_low[:, model:])
        mod_bias_grad = jnp.sum(gathered[:, model:], axis=0)
        mixed, token_grad, mod_weight_grad, mod_bias_grad, *cross_grads = rounds.finish(
            mixed, token_grad, mod_weight_grad, mod_bias_grad, *cross_grads
        )
        self_grads = rounds.four(3)

        return (
            mixed,
            token_grad,
            self_grads[0].T,
            self_grads[1].T,
            self_grads[2].T,
            self_grads[3],
            cross_grads[0].T,
            cross_grads[1].T,
            cross_grads[2].T,
            cross_grads[3],
            mlp_in_grad,
            mlp_out_grad,
            mod_weight_grad,
            mod_bias_grad,
        )

    rows = P("dp", None)
    by_col = P(None, "tensor")
    by_row = P("tensor", None)
    return jax.shard_map(
        local,
        mesh=mesh,
        in_specs=(
            rows, P("dp", None, None), P("dp"), P("dp"), P("dp"), by_col, by_col, by_col, by_row,
            by_col, by_col, by_col, by_row, by_col, by_row, by_col, P("tensor"), rows,
        ),
        out_specs=(
            rows, rows, by_col, by_col, by_col, by_row, by_col, by_col, by_col, by_row,
            by_col, by_row, by_col, P("tensor"),
        ),
        check_vma=False,
    )
```

profile of v0, /device:TPU:0, one launch (start us, length us, event | category | flops | bytes accessed | tf_op | source)
XLA Modules:
  0.0 205.8 jit_solution(15440208846958926860)
XLA Ops:
  3.8 2.4 %collective-permute-start.3 = (f32[4,1728]{1,0:T(4,128)S(1)}, f32[4,1728]{1,0:T(4,128)S(1)}, u32[]{:S(2)}, u32[]{:S(2)}) collective-permute-start(f32[4,1728]{1,0:T(4,128)S(1)} %convolution_add_fusion), channel_id=1, source_target_pairs={{0,3},{1,2},{2,1},{3,0},{4,7},{5,6},{6,5},{7,4},{8,11},{9,10},{10,... | collective-permute-start | bytes 82952 | tf_op jit(solution)/shard_map/ppermute | solution.py:680
  13.8 7.4 %self_first.1 = (bf16[256,768]{1,0:T(8,128)(2,1)S(1)}, bf16[256,768]{1,0:T(8,128)(2,1)S(1)}, bf16[3,1024,128]{2,1,0:T(8,128)(2,1)S(1)}, bf16[3,1024,128]{2,1,0:T...) custom-call(s32[8,128]{1,0:T(8,128)S(1)} %pad.8.place, ...), custom_call_target="tpu_custom_call" | custom-call | flops 1000000 | bytes 1000 | tf_op jit(solution)/shard_map/self_first/pallas_call | solution.py:89
  27.9 4.1 %self_second.1 = (bf16[256,768]{1,0:T(8,128)(2,1)S(1)}, bf16[256,768]{1,0:T(8,128)(2,1)S(1)}, bf16[3,512,128]{2,1,0:T(8,128)(2,1)S(1)}, bf16[512,192]{1,0:T(8,128)(2,1)S(1)}) custom-call(s32[8,128]{1,0:T(8,128)S(1)} %pad.8.place, bf16[3,1024,128]{2,1,0:T(8,128)(2,1)S(1)} %get-tuple-element.315.refs_0_, ...), custom_call_target="tpu_custom_call" | custom-call | flops 1000000 | bytes 1000 | tf_op jit(solution)/shard_map/self_second/pallas_call | solution.py:89
  32.0 3.8 %collective-permute-done.10.refs_2_.refs_12_ = bf16[256,768]{1,0:T(8,128)(2,1)S(1)} collective-permute-done((bf16[256,768]{1,0:T(8,128)(2,1)S(1)}, bf16[256,768]{1,0:T(8,128)(2,1)S(1)}, u32[]{:S(2)}, u32[]{:S(2)}) %collective-permute-start.10) | collective-permute-done | bytes 393248 | tf_op jit(solution)/shard_map/ppermute | solution.py:680
  41.6 7.0 %middle_first.1 = (bf16[256,768]{1,0:T(8,128)(2,1)S(1)}, bf16[256,768]{1,0:T(8,128)(2,1)S(1)}, bf16[256,768]{1,0:T(8,128)(2,1)S(1)}, bf16[256,768]{1,0:T(8,128)(...) custom-call(s32[8,128]{1,0:T(8,128)S(1)} %pad.8.place, ...), custom_call_target="tpu_custom_call" | custom-call | flops 7500000256 | bytes 1000 | tf_op jit(solution)/shard_map/middle_first/pallas_call | solution.py:89
  50.9 8.1 %middle_second.1 = (bf16[256,768]{1,0:T(8,128)(2,1)S(1)}, bf16[256,768]{1,0:T(8,128)(2,1)S(1)}, bf16[256,768]{1,0:T(8,128)(2,1)S(1)}, bf16[256,768]{1,0:T(8,128)...) custom-call(s32[8,128]{1,0:T(8,128)S(1)} %pad.8.place, ...), custom_call_target="tpu_custom_call" | custom-call | flops 7500000256 | bytes 1000 | tf_op jit(solution)/shard_map/middle_second/pallas_call | solution.py:89
  61.2 4.1 %cross_first.1 = (bf16[256,768]{1,0:T(8,128)(2,1)S(1)}, bf16[256,768]{1,0:T(8,128)(2,1)S(1)}, bf16[256,768]{1,0:T(8,128)(2,1)S(1)}, bf16[80,768]{1,0:T(8,128)(2,...) custom-call(s32[8,128]{1,0:T(8,128)S(1)} %pad.8.place, ...), custom_call_target="tpu_custom_call" | custom-call | flops 1000000 | bytes 1000 | tf_op jit(solution)/shard_map/cross_first/pallas_call | solution.py:89
  65.3 2.8 %mlp_back.1 = (bf16[2,384,768]{2,1,0:T(8,128)(2,1)S(1)}, bf16[2,384,768]{2,1,0:T(8,128)(2,1)S(1)}, bf16[2,384,768]{2,1,0:T(8,128)(2,1)S(1)}, bf16[2,384,768]{2,1,0:T(8,128)(2,1)S(1)}) custom-call(s32[8,128]{1,0:T(8,128)S(1)} %pad.8.place, bf16[256,768]{1,0:T(8,128)(2,1)S(1)} %get-tuple-element.338.refs_0_, bf16[256,768]{1,0:T(8,128)(2,1)S(1)} %get-tuple-element.343.refs_1_, ...), custom_call_target="tpu_custom_call" | custom-call | flops 1000000 | bytes 1000 | tf_op jit(solution)/shard_map/mlp_back/pallas_call | solution.py:89
  69.6 3.2 %cross_second.1 = (bf16[256,768]{1,0:T(8,128)(2,1)S(1)}, bf16[256,768]{1,0:T(8,128)(2,1)S(1)}, bf16[256,768]{1,0:T(8,128)(2,1)S(1)}, bf16[80,768]{1,0:T(8,128)(2...) custom-call(s32[8,128]{1,0:T(8,128)S(1)} %pad.8.place, ...), custom_call_target="tpu_custom_call" | custom-call | flops 4000000000 | bytes 1000 | tf_op jit(solution)/shard_map/cross_second/pallas_call | solution.py:89
  76.5 2.8 %cross_weights.1 = (bf16[2,384,768]{2,1,0:T(8,128)(2,1)S(1)}, bf16[2,384,768]{2,1,0:T(8,128)(2,1)S(1)}) custom-call(s32[8,128]{1,0:T(8,128)S(1)} %pad.8.place, bf16[256,768]{1,0:T(8,128)(2,1)S(1)} %get-tuple-element.379.refs_0_, bf16[256,768]{1,0:T(8,128)(2,1)S(1)} %get-tuple-element.380.refs_1_, bf16[256,768]{1,0:T(8,128)(2,1)S(1)} %get-tuple-element.381.refs_2_, ...), custom_call_target="tpu_custom_call" | custom-call | flops 1000000 | bytes 1000 | tf_op jit(solution)/shard_map/cross_weights/pallas_call | solution.py:89
  79.3 7.7 %self_back_first.1 = (bf16[1024,768]{1,0:T(8,128)(2,1)S(1)}, bf16[1024,192]{1,0:T(8,128)(2,1)S(1)}, bf16[3,1024,128]{2,1,0:T(8,128)(2,1)S(1)}, bf16[3,1024,128]{...) custom-call(s32[8,128]{1,0:T(8,128)S(1)} %pad.8.place, ...), custom_call_target="tpu_custom_call" | custom-call | flops 1000000 | bytes 1000 | tf_op jit(solution)/shard_map/self_back_first/pallas_call | solution.py:89
  94.3 9.5 %self_back_second.1 = (bf16[512,768]{1,0:T(8,128)(2,1)S(1)}, bf16[512,768]{1,0:T(8,128)(2,1)S(1)}, bf16[384,768]{1,0:T(8,128)(2,1)S(1)}, bf16[384,768]{1,0:T(8,128)(2,1)S(1)}) custom-call(s32[8,128]{1,0:T(8,128)S(1)} %pad.8.place, bf16[1024,768]{1,0:T(8,128)(2,1)S(1)} %get-tuple-element.409.refs_0_, bf16[1024,192]{1,0:T(8,128)(2,1)S(1)} %get-tuple-element.410.refs_1_, ...), custom_call_target="tpu_custom_call" | custom-call | flops 1000000 | bytes 1000 | tf_op jit(solution)/shard_map/self_back_second/pallas_call | solution.py:89
  112.9 10.2 %collective-permute-done.32.refs_3_ = bf16[384,768]{1,0:T(8,128)(2,1)S(1)} collective-permute-done((bf16[384,768]{1,0:T(8,128)(2,1)S(1)}, bf16[384,768]{1,0:T(8,128)(2,1)S(1)}, u32[]{:S(2)}, u32[]{:S(2)}) %collective-permute-start.32) | collective-permute-done | bytes 589856 | tf_op jit(solution)/shard_map/ppermute | solution.py:846
  125.3 4.8 %collective-permute-start.35 = (bf16[384,768]{1,0:T(8,128)(2,1)S(1)}, bf16[384,768]{1,0:T(8,128)(2,1)S(1)}, u32[]{:S(2)}, u32[]{:S(2)}) collective-permute-start(bf16[384,768]{1,0:T(8,128)(2,1)S(1)} %get-tuple-element.465), channel_id=1, source_target_pairs={{0,8},{4,12},{8,0},{12,4},{16,24},{20,28},{24,16},{28,20},{1,9},{5... | collective-permute-start | bytes 1769480 | tf_op jit(solution)/shard_map/ppermute | solution.py:850
  132.4 6.1 %collective-permute-done.36.refs_4_ = bf16[384,768]{1,0:T(8,128)(2,1)S(1)} collective-permute-done((bf16[384,768]{1,0:T(8,128)(2,1)S(1)}, bf16[384,768]{1,0:T(8,128)(2,1)S(1)}, u32[]{:S(2)}, u32[]{:S(2)}) %collective-permute-start.36) | collective-permute-done | bytes 589856 | tf_op jit(solution)/shard_map/ppermute | solution.py:846
  138.5 4.2 %collective-permute-done.35.refs_5_ = bf16[384,768]{1,0:T(8,128)(2,1)S(1)} collective-permute-done((bf16[384,768]{1,0:T(8,128)(2,1)S(1)}, bf16[384,768]{1,0:T(8,128)(2,1)S(1)}, u32[]{:S(2)}, u32[]{:S(2)}) %collective-permute-start.35) | collective-permute-done | bytes 589856 | tf_op jit(solution)/shard_map/ppermute | solution.py:850
  143.7 3.8 %collective-permute-start.39 = (bf16[384,768]{1,0:T(8,128)(2,1)S(1)}, bf16[384,768]{1,0:T(8,128)(2,1)S(1)}, u32[]{:S(2)}, u32[]{:S(2)}) collective-permute-start(bf16[384,768]{1,0:T(8,128)(2,1)S(1)} %get-tuple-element.507), channel_id=1, source_target_pairs={{0,8},{4,12},{8,0},{12,4},{16,24},{20,28},{24,16},{28,20},{1,9},{5... | collective-permute-start | bytes 1769480 | tf_op jit(solution)/shard_map/ppermute | solution.py:850
  148.8 8.0 %collective-permute-done.40.refs_1_ = bf16[384,768]{1,0:T(8,128)(2,1)S(1)} collective-permute-done((bf16[384,768]{1,0:T(8,128)(2,1)S(1)}, bf16[384,768]{1,0:T(8,128)(2,1)S(1)}, u32[]{:S(2)}, u32[]{:S(2)}) %collective-permute-start.40) | collective-permute-done | bytes 589856 | tf_op jit(solution)/shard_map/ppermute | solution.py:848
  160.7 3.8 %collective-permute-start.44 = (bf16[384,768]{1,0:T(8,128)(2,1)S(1)}, bf16[384,768]{1,0:T(8,128)(2,1)S(1)}, u32[]{:S(2)}, u32[]{:S(2)}) collective-permute-start(bf16[384,768]{1,0:T(8,128)(2,1)S(1)} %get-tuple-element.526.refs_1_), channel_id=1, source_target_pairs={{0,8},{4,12},{8,0},{12,4},{16,24},{20,28},{24,16},{28,20},{1,9},{5... | collective-permute-start | bytes 1769480 | tf_op jit(solution)/shard_map/ppermute | solution.py:850
  166.3 6.2 %collective-permute-done.46 = f32[4,2496]{1,0:T(4,128)S(1)} collective-permute-done((f32[4,2496]{1,0:T(4,128)S(1)}, f32[4,2496]{1,0:T(4,128)S(1)}, u32[]{:S(2)}, u32[]{:S(2)}) %collective-permute-start.46) | collective-permute-done | bytes 39968 | tf_op jit(solution)/shard_map/ppermute | solution.py:689
  172.6 2.1 %collective-permute-done.44.refs_2_ = bf16[384,768]{1,0:T(8,128)(2,1)S(1)} collective-permute-done((bf16[384,768]{1,0:T(8,128)(2,1)S(1)}, bf16[384,768]{1,0:T(8,128)(2,1)S(1)}, u32[]{:S(2)}, u32[]{:S(2)}) %collective-permute-start.44) | collective-permute-done | bytes 589856 | tf_op jit(solution)/shard_map/ppermute | solution.py:850
  175.5 3.7 %collective-permute-start.48 = (bf16[384,768]{1,0:T(8,128)(2,1)S(1)}, bf16[384,768]{1,0:T(8,128)(2,1)S(1)}, u32[]{:S(2)}, u32[]{:S(2)}) collective-permute-start(bf16[384,768]{1,0:T(8,128)(2,1)S(1)} %get-tuple-element.545.refs_0_), channel_id=1, source_target_pairs={{0,8},{4,12},{8,0},{12,4},{16,24},{20,28},{24,16},{28,20},{1,9},{5... | collective-permute-start | bytes 1769480 | tf_op jit(solution)/shard_map/ppermute | solution.py:850
  184.4 7.2 %collective-permute-done.50 = f32[8,2496]{1,0:T(8,128)S(1)} collective-permute-done((f32[8,2496]{1,0:T(8,128)S(1)}, f32[8,2496]{1,0:T(8,128)S(1)}, u32[]{:S(2)}, u32[]{:S(2)}) %collective-permute-start.50) | collective-permute-done | bytes 79904 | tf_op jit(solution)/shard_map/ppermute | solution.py:689
  200.6 3.3 %fusion.6 = f32[768,1728]{0,1:T(8,128)} fusion(bf16[32,2496]{1,0:T(8,128)(2,1)S(1)} %convert_element_type.171), kind=kOutput, calls=%fused_computation.22 | convolution fusion | flops 84934656 | bytes 5468160 | tf_op jit(solution)/shard_map/dot_general | solution.py:30
  (192 shorter events, 78.1 us)
Async XLA Ops:
  7.2 13.9 %collective-permute-start.4 = (bf16[192,768]{1,0:T(8,128)(2,1)}, bf16[192,768]{1,0:T(8,128)(2,1)}, u32[]{:S(2)}, u32[]{:S(2)}) collective-permute-start(bf16[192,768]{1,0:T(8,128)(2,1)} %pad_maximum_fusion.2), channel_id=1, source_target_pairs={{0,2},{1,3},{2,0},{3,1},{4,6},{5,7},{6,4},{7,5},{8,10},{9,11},{10,... | collective-permute-start | bytes 884744 | tf_op jit(solution)/shard_map/ppermute | solution.py:680
  72.8 16.2 %collective-permute-start.24 = (bf16[2,384,768]{2,1,0:T(8,128)(2,1)S(1)}, bf16[2,384,768]{2,1,0:T(8,128)(2,1)S(1)}, u32[]{:S(2)}, u32[]{:S(2)}) collective-permute-start(bf16[2,384,768]{2,1,0:T(8,128)(2,1)S(1)} %get-tuple-element.400), channel_id=1, source_target_pairs={{0,1},{1,0},{2,3},{3,2},{4,5},{5,4},{6,7},{7,6},{8,9},{9,8},{10,11... | collective-permute-start | bytes 3538952 | tf_op jit(solution)/shard_map/ppermute | solution.py:680
  73.2 15.8 %collective-permute-start.22 = (bf16[384,768]{1,0:T(8,128)(2,1)S(1)}, bf16[384,768]{1,0:T(8,128)(2,1)S(1)}, u32[]{:S(2)}, u32[]{:S(2)}) collective-permute-start(bf16[384,768]{1,0:T(8,128)(2,1)S(1)} %get-tuple-element.590), channel_id=1, source_target_pairs={{0,4},{4,0},{8,12},{12,8},{16,20},{20,16},{24,28},{28,24},{1,5},{5... | collective-permute-start | bytes 1769480 | tf_op jit(solution)/shard_map/ppermute | solution.py:846
  75.1 14.3 %collective-permute-start.25 = (bf16[256,768]{1,0:T(8,128)(2,1)S(1)}, bf16[256,768]{1,0:T(8,128)(2,1)S(1)}, u32[]{:S(2)}, u32[]{:S(2)}) collective-permute-start(bf16[256,768]{1,0:T(8,128)(2,1)S(1)} %get-tuple-element.402.refs_1_), channel_id=1, source_target_pairs={{0,2},{1,3},{2,0},{3,1},{4,6},{5,7},{6,4},{7,5},{8,10},{9,11},{10,... | collective-permute-start | bytes 1179656 | tf_op jit(solution)/shard_map/ppermute | solution.py:680
  89.5 17.1 %collective-permute-start.26 = (bf16[2,384,768]{2,1,0:T(8,128)(2,1)S(1)}, bf16[2,384,768]{2,1,0:T(8,128)(2,1)S(1)}, u32[]{:S(2)}, u32[]{:S(2)}) collective-permute-start(bf16[2,384,768]{2,1,0:T(8,128)(2,1)S(1)} %get-tuple-element.419), channel_id=1, source_target_pairs={{0,1},{1,0},{2,3},{3,2},{4,5},{5,4},{6,7},{7,6},{8,9},{9,8},{10,11... | collective-permute-start | bytes 3538952 | tf_op jit(solution)/shard_map/ppermute | solution.py:680
  89.6 15.7 %collective-permute-start.28 = (bf16[384,768]{1,0:T(8,128)(2,1)S(1)}, bf16[384,768]{1,0:T(8,128)(2,1)S(1)}, u32[]{:S(2)}, u32[]{:S(2)}) collective-permute-start(bf16[384,768]{1,0:T(8,128)(2,1)S(1)} %get-tuple-element.421), channel_id=1, source_target_pairs={{0,4},{4,0},{8,12},{12,8},{16,20},{20,16},{24,28},{28,24},{1,5},{5... | collective-permute-start | bytes 1769480 | tf_op jit(solution)/shard_map/ppermute | solution.py:846
  91.2 15.4 %collective-permute-start.27 = (bf16[384,768]{1,0:T(8,128)(2,1)S(1)}, bf16[384,768]{1,0:T(8,128)(2,1)S(1)}, u32[]{:S(2)}, u32[]{:S(2)}) collective-permute-start(bf16[384,768]{1,0:T(8,128)(2,1)S(1)} %advance.7.refs_1_), channel_id=1, source_target_pairs={{0,8},{4,12},{8,0},{12,4},{16,24},{20,28},{24,16},{28,20},{1,9},{5... | collective-permute-start | bytes 1769480 | tf_op jit(solution)/shard_map/ppermute | solution.py:850
  92.8 14.1 %collective-permute-start.29 = (bf16[256,768]{1,0:T(8,128)(2,1)S(1)}, bf16[256,768]{1,0:T(8,128)(2,1)S(1)}, u32[]{:S(2)}, u32[]{:S(2)}) collective-permute-start(bf16[256,768]{1,0:T(8,128)(2,1)S(1)} %get-tuple-element.426.refs_2_), channel_id=1, source_target_pairs={{0,2},{1,3},{2,0},{3,1},{4,6},{5,7},{6,4},{7,5},{8,10},{9,11},{10,... | collective-permute-start | bytes 1179656 | tf_op jit(solution)/shard_map/ppermute | solution.py:680
  107.4 15.7 %collective-permute-start.32 = (bf16[384,768]{1,0:T(8,128)(2,1)S(1)}, bf16[384,768]{1,0:T(8,128)(2,1)S(1)}, u32[]{:S(2)}, u32[]{:S(2)}) collective-permute-start(bf16[384,768]{1,0:T(8,128)(2,1)S(1)} %get-tuple-element.437), channel_id=1, source_target_pairs={{0,4},{4,0},{8,12},{12,8},{16,20},{20,16},{24,28},{28,24},{1,5},{5... | collective-permute-start | bytes 1769480 | tf_op jit(solution)/shard_map/ppermute | solution.py:846
  107.9 15.4 %collective-permute-start.31 = (bf16[384,768]{1,0:T(8,128)(2,1)S(1)}, bf16[384,768]{1,0:T(8,128)(2,1)S(1)}, u32[]{:S(2)}, u32[]{:S(2)}) collective-permute-start(bf16[384,768]{1,0:T(8,128)(2,1)S(1)} %get-tuple-element.435.refs_1_), channel_id=1, source_target_pairs={{0,8},{4,12},{8,0},{12,4},{16,24},{20,28},{24,16},{28,20},{1,9},{5... | collective-permute-start | bytes 1769480 | tf_op jit(solution)/shard_map/ppermute | solution.py:850
  109.6 13.7 %collective-permute-start.30 = (bf16[384,768]{1,0:T(8,128)(2,1)S(1)}, bf16[384,768]{1,0:T(8,128)(2,1)S(1)}, u32[]{:S(2)}, u32[]{:S(2)}) collective-permute-start(bf16[384,768]{1,0:T(8,128)(2,1)S(1)} %get-tuple-element.436.refs_2_), channel_id=1, source_target_pairs={{8,16},{12,20},{16,8},{20,12},{9,17},{13,21},{17,9},{21,13},{10,18... | collective-permute-start | bytes 1769480 | tf_op jit(solution)/shard_map/ppermute | solution.py:852
  110.5 20.5 %collective-permute-start.37 = (bf16[512,768]{1,0:T(8,128)(2,1)S(1)}, bf16[512,768]{1,0:T(8,128)(2,1)S(1)}, u32[]{:S(2)}, u32[]{:S(2)}) collective-permute-start(bf16[512,768]{1,0:T(8,128)(2,1)S(1)} %add_convert_fusion.refs_1_), channel_id=1, source_target_pairs={{0,2},{1,3},{2,0},{3,1},{4,6},{5,7},{6,4},{7,5},{8,10},{9,11},{10,... | collective-permute-start | bytes 2359304 | tf_op jit(solution)/shard_map/ppermute | solution.py:680
  123.7 14.8 %collective-permute-start.36 = (bf16[384,768]{1,0:T(8,128)(2,1)S(1)}, bf16[384,768]{1,0:T(8,128)(2,1)S(1)}, u32[]{:S(2)}, u32[]{:S(2)}) collective-permute-start(bf16[384,768]{1,0:T(8,128)(2,1)S(1)} %get-tuple-element.466), channel_id=1, source_target_pairs={{0,4},{4,0},{8,12},{12,8},{16,20},{20,16},{24,28},{28,24},{1,5},{5... | collective-permute-start | bytes 1769480 | tf_op jit(solution)/shard_map/ppermute | solution.py:846
  125.3 17.3 %collective-permute-start.35 = (bf16[384,768]{1,0:T(8,128)(2,1)S(1)}, bf16[384,768]{1,0:T(8,128)(2,1)S(1)}, u32[]{:S(2)}, u32[]{:S(2)}) collective-permute-start(bf16[384,768]{1,0:T(8,128)(2,1)S(1)} %get-tuple-element.465), channel_id=1, source_target_pairs={{0,8},{4,12},{8,0},{12,4},{16,24},{20,28},{24,16},{28,20},{1,9},{5... | collective-permute-start | bytes 1769480 | tf_op jit(solution)/shard_map/ppermute | solution.py:850
  130.1 12.5 %collective-permute-start.34 = (bf16[384,768]{1,0:T(8,128)(2,1)S(1)}, bf16[384,768]{1,0:T(8,128)(2,1)S(1)}, u32[]{:S(2)}, u32[]{:S(2)}) collective-permute-start(bf16[384,768]{1,0:T(8,128)(2,1)S(1)} %get-tuple-element.463.refs_2_), channel_id=1, source_target_pairs={{8,16},{12,20},{16,8},{20,12},{9,17},{13,21},{17,9},{21,13},{10,18... | collective-permute-start | bytes 1769480 | tf_op jit(solution)/shard_map/ppermute | solution.py:852
  143.2 13.7 %collective-permute-start.40 = (bf16[384,768]{1,0:T(8,128)(2,1)S(1)}, bf16[384,768]{1,0:T(8,128)(2,1)S(1)}, u32[]{:S(2)}, u32[]{:S(2)}) collective-permute-start(bf16[384,768]{1,0:T(8,128)(2,1)S(1)} %get-tuple-element.508.refs_0_), channel_id=1, source_target_pairs={{0,4},{4,0},{8,12},{12,8},{16,20},{20,16},{24,28},{28,24},{1,5},{5... | collective-permute-start | bytes 1769480 | tf_op jit(solution)/shard_map/ppermute | solution.py:848
  143.7 15.2 %collective-permute-start.39 = (bf16[384,768]{1,0:T(8,128)(2,1)S(1)}, bf16[384,768]{1,0:T(8,128)(2,1)S(1)}, u32[]{:S(2)}, u32[]{:S(2)}) collective-permute-start(bf16[384,768]{1,0:T(8,128)(2,1)S(1)} %get-tuple-element.507), channel_id=1, source_target_pairs={{0,8},{4,12},{8,0},{12,4},{16,24},{20,28},{24,16},{28,20},{1,9},{5... | collective-permute-start | bytes 1769480 | tf_op jit(solution)/shard_map/ppermute | solution.py:850
  159.1 13.4 %collective-permute-start.45 = (bf16[384,768]{1,0:T(8,128)(2,1)S(1)}, bf16[384,768]{1,0:T(8,128)(2,1)S(1)}, u32[]{:S(2)}, u32[]{:S(2)}) collective-permute-start(bf16[384,768]{1,0:T(8,128)(2,1)S(1)} %get-tuple-element.527.refs_0_), channel_id=1, source_target_pairs={{0,4},{4,0},{8,12},{12,8},{16,20},{20,16},{24,28},{28,24},{1,5},{5... | collective-permute-start | bytes 1769480 | tf_op jit(solution)/shard_map/ppermute | solution.py:848
  160.7 14.0 %collective-permute-start.44 = (bf16[384,768]{1,0:T(8,128)(2,1)S(1)}, bf16[384,768]{1,0:T(8,128)(2,1)S(1)}, u32[]{:S(2)}, u32[]{:S(2)}) collective-permute-start(bf16[384,768]{1,0:T(8,128)(2,1)S(1)} %get-tuple-element.526.refs_1_), channel_id=1, source_target_pairs={{0,8},{4,12},{8,0},{12,4},{16,24},{20,28},{24,16},{28,20},{1,9},{5... | collective-permute-start | bytes 1769480 | tf_op jit(solution)/shard_map/ppermute | solution.py:850
  174.9 16.8 %collective-permute-start.49 = (bf16[384,768]{1,0:T(8,128)(2,1)S(1)}, bf16[384,768]{1,0:T(8,128)(2,1)S(1)}, u32[]{:S(2)}, u32[]{:S(2)}) collective-permute-start(bf16[384,768]{1,0:T(8,128)(2,1)S(1)} %get-tuple-element.546.refs_0_), channel_id=1, source_target_pairs={{0,4},{4,0},{8,12},{12,8},{16,20},{20,16},{24,28},{28,24},{1,5},{5... | collective-permute-start | bytes 1769480 | tf_op jit(solution)/shard_map/ppermute | solution.py:848
  175.5 16.2 %collective-permute-start.48 = (bf16[384,768]{1,0:T(8,128)(2,1)S(1)}, bf16[384,768]{1,0:T(8,128)(2,1)S(1)}, u32[]{:S(2)}, u32[]{:S(2)}) collective-permute-start(bf16[384,768]{1,0:T(8,128)(2,1)S(1)} %get-tuple-element.545.refs_0_), channel_id=1, source_target_pairs={{0,8},{4,12},{8,0},{12,4},{16,24},{20,28},{24,16},{28,20},{1,9},{5... | collective-permute-start | bytes 1769480 | tf_op jit(solution)/shard_map/ppermute | solution.py:850
  179.2 12.5 %collective-permute-start.50 = (f32[8,2496]{1,0:T(8,128)S(1)}, f32[8,2496]{1,0:T(8,128)S(1)}, u32[]{:S(2)}, u32[]{:S(2)}) collective-permute-start(f32[8,2496]{1,0:T(8,128)S(1)} %pad_maximum_fusion.5), channel_id=1, source_target_pairs={{0,8},{4,12},{8,0},{12,4},{16,24},{20,28},{24,16},{28,20},{1,9},{5... | collective-permute-start | bytes 239624 | tf_op jit(solution)/shard_map/ppermute | solution.py:689
  179.2 12.5 %collective-permute-start.51 = (bf16[256,768]{1,0:T(8,128)(2,1)S(1)}, bf16[256,768]{1,0:T(8,128)(2,1)S(1)}, u32[]{:S(2)}, u32[]{:S(2)}) collective-permute-start(bf16[256,768]{1,0:T(8,128)(2,1)S(1)} %get-tuple-element.550.refs_0_), channel_id=1, source_target_pairs={{0,1},{1,0},{2,3},{3,2},{4,5},{5,4},{6,7},{7,6},{8,9},{9,8},{10,11... | collective-permute-start | bytes 1179656 | tf_op jit(solution)/shard_map/ppermute | solution.py:680
  179.2 12.5 %collective-permute-start.52 = (bf16[256,768]{1,0:T(8,128)(2,1)S(1)}, bf16[256,768]{1,0:T(8,128)(2,1)S(1)}, u32[]{:S(2)}, u32[]{:S(2)}) collective-permute-start(bf16[256,768]{1,0:T(8,128)(2,1)S(1)} %get-tuple-element.551.refs_1_), channel_id=1, source_target_pairs={{0,1},{1,0},{2,3},{3,2},{4,5},{5,4},{6,7},{7,6},{8,9},{9,8},{10,11... | collective-permute-start | bytes 1179656 | tf_op jit(solution)/shard_map/ppermute | solution.py:680
  (52 other events, 330.9 us)
where the time goes:
time: 208 us; the launch traced here: 206 us
  Pallas kernels  73.4 us (35%)
  waiting for transfers between devices  63.4 us (30%)
  starting transfers between devices  55.9 us (27%)
  other arithmetic  5.17 us (2%)
  matrix products  4.06 us (2%)
  local copies, waits for them, and re-layouts  2.28 us (1%)
    pallas_call x28, Pallas kernels, run(): pl.pallas_call(wrapped, name=getattr(kernel, '__name__', 'advance'), out_...  73.4 us
    ppermute x33, starting transfers between devices, tensor_swap(): lax.ppermute(value, 'tensor', [(i, i ^ flip) for i in range(n_tensor)])  20.5 us
    ppermute x4, waiting for transfers between devices, start(): self.got['row'] = lax.ppermute(chain[1], 'dp', across)  19.7 us
    ppermute x6, starting transfers between devices, start(): self.got['column'] = lax.ppermute(self.column_send, 'dp', neighbours)  19.4 us
    ppermute x4, waiting for transfers between devices, dp_swap(): return lax.ppermute(value, 'dp', [(i, i ^ flip) for i in range(n_dp)])  15.5 us
    ppermute x33, waiting for transfers between devices, tensor_swap(): lax.ppermute(value, 'tensor', [(i, i ^ flip) for i in range(n_tensor)])  10.3 us
    ppermute x6, waiting for transfers between devices, start(): self.got['column'] = lax.ppermute(self.column_send, 'dp', neighbours)  9.79 us
    ppermute x4, waiting for transfers between devices, start(): self.got['last'] = lax.ppermute(self.values['e'], 'dp', across)  8.06 us
  transfers between devices with their start and end apart: 55, of which 21 were waited for; matrix products, arithmetic and copies ran while one was open for 5% of the time, Pallas kernels for 34%

commit v1 on v0

--- a/solution.py
+++ b/solution.py
@@ -383,11 +383,8 @@
                 part = wide[u * text_rows : (u + 1) * text_rows, :] * masks[u]
                 total = part if total is None else total + part
             out[:, cols] = total.astype(BF16)
-    if chunk:
-        for quad in range(model // (4 * HEAD)):
-            by_quad(quad)
-    else:
-        pl.loop(0, model // (4 * HEAD))(by_quad)
+    for quad in range(model // (4 * HEAD)):
+        by_quad(quad)
     h2g = dot_nn(dq_out[...], cqt[...])
     normed, inverse = normalize(x1)
     sums[1:2, :] = column_sum(h2g)

time: 208 us -> 209 us (level)
  transfers between devices with their start and end apart: 55 -> 55, of which waited for: 21 -> 21; matrix products, arithmetic and copies ran while one was open for 5% -> 5% of each run, Pallas kernels for 34% -> 33%
where the time goes in v1:
time: 209 us; the launch traced here: 206 us
  Pallas kernels  72 us (34%)
  waiting for transfers between devices  64.8 us (31%)
  starting transfers between devices  55.9 us (27%)
  other arithmetic  5.57 us (3%)
  matrix products  4.07 us (2%)
  local copies, waits for them, and re-layouts  2.28 us (1%)
    pallas_call x28, Pallas kernels, run(): pl.pallas_call(wrapped, name=getattr(kernel, '__name__', 'advance'), out_...  72 us
    ppermute x33, starting transfers between devices, tensor_swap(): lax.ppermute(value, 'tensor', [(i, i ^ flip) for i in range(n_tensor)])  20.5 us
    ppermute x4, waiting for transfers between devices, start(): self.got['row'] = lax.ppermute(chain[1], 'dp', across)  20.1 us
    ppermute x6, starting transfers between devices, start(): self.got['column'] = lax.ppermute(self.column_send, 'dp', neighbours)  19.4 us
    ppermute x4, waiting for transfers between devices, dp_swap(): return lax.ppermute(value, 'dp', [(i, i ^ flip) for i in range(n_dp)])  15.5 us
    ppermute x33, waiting for transfers between devices, tensor_swap(): lax.ppermute(value, 'tensor', [(i, i ^ flip) for i in range(n_tensor)])  11.3 us
    ppermute x6, waiting for transfers between devices, start(): self.got['column'] = lax.ppermute(self.column_send, 'dp', neighbours)  9.79 us
    ppermute x4, waiting for transfers between devices, start(): self.got['last'] = lax.ppermute(self.values['e'], 'dp', across)  8.06 us
  transfers between devices with their start and end apart: 55, of which 21 were waited for; matrix products, arithmetic and copies ran while one was open for 5% of the time, Pallas kernels for 33%

profile of v1, /device:TPU:0, one launch (start us, length us, event | category | flops | bytes accessed | tf_op | source)
XLA Modules:
  0.0 206.2 jit_solution(14686359920524945386)
XLA Ops:
  3.8 2.4 %collective-permute-start.3 = (f32[4,1728]{1,0:T(4,128)S(1)}, f32[4,1728]{1,0:T(4,128)S(1)}, u32[]{:S(2)}, u32[]{:S(2)}) collective-permute-start(f32[4,1728]{1,0:T(4,128)S(1)} %convolution_add_fusion), channel_id=1, source_target_pairs={{0,3},{1,2},{2,1},{3,0},{4,7},{5,6},{6,5},{7,4},{8,11},{9,10},{10,... | collective-permute-start | bytes 82952 | tf_op jit(solution)/shard_map/ppermute | solution.py:677
  13.8 7.4 %self_first.1 = (bf16[256,768]{1,0:T(8,128)(2,1)S(1)}, bf16[256,768]{1,0:T(8,128)(2,1)S(1)}, bf16[3,1024,128]{2,1,0:T(8,128)(2,1)S(1)}, bf16[3,1024,128]{2,1,0:T...) custom-call(s32[8,128]{1,0:T(8,128)S(1)} %pad.8.place, ...), custom_call_target="tpu_custom_call" | custom-call | flops 1000000 | bytes 1000 | tf_op jit(solution)/shard_map/self_first/pallas_call | solution.py:89
  27.9 4.1 %self_second.1 = (bf16[256,768]{1,0:T(8,128)(2,1)S(1)}, bf16[256,768]{1,0:T(8,128)(2,1)S(1)}, bf16[3,512,128]{2,1,0:T(8,128)(2,1)S(1)}, bf16[512,192]{1,0:T(8,128)(2,1)S(1)}) custom-call(s32[8,128]{1,0:T(8,128)S(1)} %pad.8.place, bf16[3,1024,128]{2,1,0:T(8,128)(2,1)S(1)} %get-tuple-element.315.refs_0_, ...), custom_call_target="tpu_custom_call" | custom-call | flops 1000000 | bytes 1000 | tf_op jit(solution)/shard_map/self_second/pallas_call | solution.py:89
  32.0 3.8 %collective-permute-done.10.refs_2_.refs_12_ = bf16[256,768]{1,0:T(8,128)(2,1)S(1)} collective-permute-done((bf16[256,768]{1,0:T(8,128)(2,1)S(1)}, bf16[256,768]{1,0:T(8,128)(2,1)S(1)}, u32[]{:S(2)}, u32[]{:S(2)}) %collective-permute-start.10) | collective-permute-done | bytes 393248 | tf_op jit(solution)/shard_map/ppermute | solution.py:677
  41.6 7.0 %middle_first.1 = (bf16[256,768]{1,0:T(8,128)(2,1)S(1)}, bf16[256,768]{1,0:T(8,128)(2,1)S(1)}, bf16[256,768]{1,0:T(8,128)(2,1)S(1)}, bf16[256,768]{1,0:T(8,128)(...) custom-call(s32[8,128]{1,0:T(8,128)S(1)} %pad.8.place, ...), custom_call_target="tpu_custom_call" | custom-call | flops 7500000256 | bytes 1000 | tf_op jit(solution)/shard_map/middle_first/pallas_call | solution.py:89
  50.9 8.1 %middle_second.1 = (bf16[256,768]{1,0:T(8,128)(2,1)S(1)}, bf16[256,768]{1,0:T(8,128)(2,1)S(1)}, bf16[256,768]{1,0:T(8,128)(2,1)S(1)}, bf16[256,768]{1,0:T(8,128)...) custom-call(s32[8,128]{1,0:T(8,128)S(1)} %pad.8.place, ...), custom_call_target="tpu_custom_call" | custom-call | flops 7500000256 | bytes 1000 | tf_op jit(solution)/shard_map/middle_second/pallas_call | solution.py:89
  61.2 3.1 %cross_first.1 = (bf16[256,768]{1,0:T(8,128)(2,1)S(1)}, bf16[256,768]{1,0:T(8,128)(2,1)S(1)}, bf16[256,768]{1,0:T(8,128)(2,1)S(1)}, bf16[80,768]{1,0:T(8,128)(2,...) custom-call(s32[8,128]{1,0:T(8,128)S(1)} %pad.8.place, ...), custom_call_target="tpu_custom_call" | custom-call | flops 1000000 | bytes 1000 | tf_op jit(solution)/shard_map/cross_first/pallas_call | solution.py:89
  64.3 2.8 %mlp_back.1 = (bf16[2,384,768]{2,1,0:T(8,128)(2,1)S(1)}, bf16[2,384,768]{2,1,0:T(8,128)(2,1)S(1)}, bf16[2,384,768]{2,1,0:T(8,128)(2,1)S(1)}, bf16[2,384,768]{2,1,0:T(8,128)(2,1)S(1)}) custom-call(s32[8,128]{1,0:T(8,128)S(1)} %pad.8.place, bf16[256,768]{1,0:T(8,128)(2,1)S(1)} %get-tuple-element.338.refs_0_, bf16[256,768]{1,0:T(8,128)(2,1)S(1)} %get-tuple-element.343.refs_1_, ...), custom_call_target="tpu_custom_call" | custom-call | flops 1000000 | bytes 1000 | tf_op jit(solution)/shard_map/mlp_back/pallas_call | solution.py:89
  69.6 3.2 %cross_second.1 = (bf16[256,768]{1,0:T(8,128)(2,1)S(1)}, bf16[256,768]{1,0:T(8,128)(2,1)S(1)}, bf16[256,768]{1,0:T(8,128)(2,1)S(1)}, bf16[80,768]{1,0:T(8,128)(2...) custom-call(s32[8,128]{1,0:T(8,128)S(1)} %pad.8.place, ...), custom_call_target="tpu_custom_call" | custom-call | flops 4000000000 | bytes 1000 | tf_op jit(solution)/shard_map/cross_second/pallas_call | solution.py:89
  76.9 2.3 %cross_weights.1 = (bf16[2,384,768]{2,1,0:T(8,128)(2,1)S(1)}, bf16[2,384,768]{2,1,0:T(8,128)(2,1)S(1)}) custom-call(s32[8,128]{1,0:T(8,128)S(1)} %pad.8.place, bf16[256,768]{1,0:T(8,128)(2,1)S(1)} %get-tuple-element.379.refs_0_, bf16[256,768]{1,0:T(8,128)(2,1)S(1)} %get-tuple-element.380.refs_1_, bf16[256,768]{1,0:T(8,128)(2,1)S(1)} %get-tuple-element.381.refs_2_, ...), custom_call_target="tpu_custom_call" | custom-call | flops 1000000 | bytes 1000 | tf_op jit(solution)/shard_map/cross_weights/pallas_call | solution.py:89
  79.3 7.7 %self_back_first.1 = (bf16[1024,768]{1,0:T(8,128)(2,1)S(1)}, bf16[1024,192]{1,0:T(8,128)(2,1)S(1)}, bf16[3,1024,128]{2,1,0:T(8,128)(2,1)S(1)}, bf16[3,1024,128]{...) custom-call(s32[8,128]{1,0:T(8,128)S(1)} %pad.8.place, ...), custom_call_target="tpu_custom_call" | custom-call | flops 1000000 | bytes 1000 | tf_op jit(solution)/shard_map/self_back_first/pallas_call | solution.py:89
  87.0 2.4 %collective-permute-done.22.refs_1_ = bf16[384,768]{1,0:T(8,128)(2,1)S(1)} collective-permute-done((bf16[384,768]{1,0:T(8,128)(2,1)S(1)}, bf16[384,768]{1,0:T(8,128)(2,1)S(1)}, u32[]{:S(2)}, u32[]{:S(2)}) %collective-permute-start.22) | collective-permute-done | bytes 589856 | tf_op jit(solution)/shard_map/ppermute | solution.py:843
  94.7 9.5 %self_back_second.1 = (bf16[512,768]{1,0:T(8,128)(2,1)S(1)}, bf16[512,768]{1,0:T(8,128)(2,1)S(1)}, bf16[384,768]{1,0:T(8,128)(2,1)S(1)}, bf16[384,768]{1,0:T(8,128)(2,1)S(1)}) custom-call(s32[8,128]{1,0:T(8,128)S(1)} %pad.8.place, bf16[1024,768]{1,0:T(8,128)(2,1)S(1)} %get-tuple-element.409.refs_0_, bf16[1024,192]{1,0:T(8,128)(2,1)S(1)} %get-tuple-element.410.refs_1_, ...), custom_call_target="tpu_custom_call" | custom-call | flops 1000000 | bytes 1000 | tf_op jit(solution)/shard_map/self_back_second/pallas_call | solution.py:89
  113.3 10.2 %collective-permute-done.32.refs_3_ = bf16[384,768]{1,0:T(8,128)(2,1)S(1)} collective-permute-done((bf16[384,768]{1,0:T(8,128)(2,1)S(1)}, bf16[384,768]{1,0:T(8,128)(2,1)S(1)}, u32[]{:S(2)}, u32[]{:S(2)}) %collective-permute-start.32) | collective-permute-done | bytes 589856 | tf_op jit(solution)/shard_map/ppermute | solution.py:843
  125.7 4.8 %collective-permute-start.35 = (bf16[384,768]{1,0:T(8,128)(2,1)S(1)}, bf16[384,768]{1,0:T(8,128)(2,1)S(1)}, u32[]{:S(2)}, u32[]{:S(2)}) collective-permute-start(bf16[384,768]{1,0:T(8,128)(2,1)S(1)} %get-tuple-element.465), channel_id=1, source_target_pairs={{0,8},{4,12},{8,0},{12,4},{16,24},{20,28},{24,16},{28,20},{1,9},{5... | collective-permute-start | bytes 1769480 | tf_op jit(solution)/shard_map/ppermute | solution.py:847
  132.8 6.1 %collective-permute-done.36.refs_4_ = bf16[384,768]{1,0:T(8,128)(2,1)S(1)} collective-permute-done((bf16[384,768]{1,0:T(8,128)(2,1)S(1)}, bf16[384,768]{1,0:T(8,128)(2,1)S(1)}, u32[]{:S(2)}, u32[]{:S(2)}) %collective-permute-start.36) | collective-permute-done | bytes 589856 | tf_op jit(solution)/shard_map/ppermute | solution.py:843
  138.9 4.2 %collective-permute-done.35.refs_5_ = bf16[384,768]{1,0:T(8,128)(2,1)S(1)} collective-permute-done((bf16[384,768]{1,0:T(8,128)(2,1)S(1)}, bf16[384,768]{1,0:T(8,128)(2,1)S(1)}, u32[]{:S(2)}, u32[]{:S(2)}) %collective-permute-start.35) | collective-permute-done | bytes 589856 | tf_op jit(solution)/shard_map/ppermute | solution.py:847
  144.1 3.8 %collective-permute-start.39 = (bf16[384,768]{1,0:T(8,128)(2,1)S(1)}, bf16[384,768]{1,0:T(8,128)(2,1)S(1)}, u32[]{:S(2)}, u32[]{:S(2)}) collective-permute-start(bf16[384,768]{1,0:T(8,128)(2,1)S(1)} %get-tuple-element.507), channel_id=1, source_target_pairs={{0,8},{4,12},{8,0},{12,4},{16,24},{20,28},{24,16},{28,20},{1,9},{5... | collective-permute-start | bytes 1769480 | tf_op jit(solution)/shard_map/ppermute | solution.py:847
  149.2 8.1 %collective-permute-done.40.refs_1_ = bf16[384,768]{1,0:T(8,128)(2,1)S(1)} collective-permute-done((bf16[384,768]{1,0:T(8,128)(2,1)S(1)}, bf16[384,768]{1,0:T(8,128)(2,1)S(1)}, u32[]{:S(2)}, u32[]{:S(2)}) %collective-permute-start.40) | collective-permute-done | bytes 589856 | tf_op jit(solution)/shard_map/ppermute | solution.py:845
  161.1 3.8 %collective-permute-start.44 = (bf16[384,768]{1,0:T(8,128)(2,1)S(1)}, bf16[384,768]{1,0:T(8,128)(2,1)S(1)}, u32[]{:S(2)}, u32[]{:S(2)}) collective-permute-start(bf16[384,768]{1,0:T(8,128)(2,1)S(1)} %get-tuple-element.526.refs_1_), channel_id=1, source_target_pairs={{0,8},{4,12},{8,0},{12,4},{16,24},{20,28},{24,16},{28,20},{1,9},{5... | collective-permute-start | bytes 1769480 | tf_op jit(solution)/shard_map/ppermute | solution.py:847
  166.7 6.2 %collective-permute-done.46 = f32[4,2496]{1,0:T(4,128)S(1)} collective-permute-done((f32[4,2496]{1,0:T(4,128)S(1)}, f32[4,2496]{1,0:T(4,128)S(1)}, u32[]{:S(2)}, u32[]{:S(2)}) %collective-permute-start.46) | collective-permute-done | bytes 39968 | tf_op jit(solution)/shard_map/ppermute | solution.py:686
  175.9 3.7 %collective-permute-start.48 = (bf16[384,768]{1,0:T(8,128)(2,1)S(1)}, bf16[384,768]{1,0:T(8,128)(2,1)S(1)}, u32[]{:S(2)}, u32[]{:S(2)}) collective-permute-start(bf16[384,768]{1,0:T(8,128)(2,1)S(1)} %get-tuple-element.545.refs_0_), channel_id=1, source_target_pairs={{0,8},{4,12},{8,0},{12,4},{16,24},{20,28},{24,16},{28,20},{1,9},{5... | collective-permute-start | bytes 1769480 | tf_op jit(solution)/shard_map/ppermute | solution.py:847
  184.8 7.2 %collective-permute-done.50 = f32[8,2496]{1,0:T(8,128)S(1)} collective-permute-done((f32[8,2496]{1,0:T(8,128)S(1)}, f32[8,2496]{1,0:T(8,128)S(1)}, u32[]{:S(2)}, u32[]{:S(2)}) %collective-permute-start.50) | collective-permute-done | bytes 79904 | tf_op jit(solution)/shard_map/ppermute | solution.py:686
  201.0 3.3 %fusion.6 = f32[768,1728]{0,1:T(8,128)} fusion(bf16[32,2496]{1,0:T(8,128)(2,1)S(1)} %convert_element_type.171), kind=kOutput, calls=%fused_computation.22 | convolution fusion | flops 84934656 | bytes 5468160 | tf_op jit(solution)/shard_map/dot_general | solution.py:30
  (192 shorter events, 79.6 us)
Async XLA Ops:
  7.2 13.9 %collective-permute-start.4 = (bf16[192,768]{1,0:T(8,128)(2,1)}, bf16[192,768]{1,0:T(8,128)(2,1)}, u32[]{:S(2)}, u32[]{:S(2)}) collective-permute-start(bf16[192,768]{1,0:T(8,128)(2,1)} %pad_maximum_fusion.2), channel_id=1, source_target_pairs={{0,2},{1,3},{2,0},{3,1},{4,6},{5,7},{6,4},{7,5},{8,10},{9,11},{10,... | collective-permute-start | bytes 884744 | tf_op jit(solution)/shard_map/ppermute | solution.py:677
  72.8 16.6 %collective-permute-start.24 = (bf16[2,384,768]{2,1,0:T(8,128)(2,1)S(1)}, bf16[2,384,768]{2,1,0:T(8,128)(2,1)S(1)}, u32[]{:S(2)}, u32[]{:S(2)}) collective-permute-start(bf16[2,384,768]{2,1,0:T(8,128)(2,1)S(1)} %get-tuple-element.400), channel_id=1, source_target_pairs={{0,1},{1,0},{2,3},{3,2},{4,5},{5,4},{6,7},{7,6},{8,9},{9,8},{10,11... | collective-permute-start | bytes 3538952 | tf_op jit(solution)/shard_map/ppermute | solution.py:677
  73.6 15.8 %collective-permute-start.22 = (bf16[384,768]{1,0:T(8,128)(2,1)S(1)}, bf16[384,768]{1,0:T(8,128)(2,1)S(1)}, u32[]{:S(2)}, u32[]{:S(2)}) collective-permute-start(bf16[384,768]{1,0:T(8,128)(2,1)S(1)} %get-tuple-element.590), channel_id=1, source_target_pairs={{0,4},{4,0},{8,12},{12,8},{16,20},{20,16},{24,28},{28,24},{1,5},{5... | collective-permute-start | bytes 1769480 | tf_op jit(solution)/shard_map/ppermute | solution.py:843
  75.5 14.3 %collective-permute-start.25 = (bf16[256,768]{1,0:T(8,128)(2,1)S(1)}, bf16[256,768]{1,0:T(8,128)(2,1)S(1)}, u32[]{:S(2)}, u32[]{:S(2)}) collective-permute-start(bf16[256,768]{1,0:T(8,128)(2,1)S(1)} %get-tuple-element.402.refs_1_), channel_id=1, source_target_pairs={{0,2},{1,3},{2,0},{3,1},{4,6},{5,7},{6,4},{7,5},{8,10},{9,11},{10,... | collective-permute-start | bytes 1179656 | tf_op jit(solution)/shard_map/ppermute | solution.py:677
  89.9 17.1 %collective-permute-start.26 = (bf16[2,384,768]{2,1,0:T(8,128)(2,1)S(1)}, bf16[2,384,768]{2,1,0:T(8,128)(2,1)S(1)}, u32[]{:S(2)}, u32[]{:S(2)}) collective-permute-start(bf16[2,384,768]{2,1,0:T(8,128)(2,1)S(1)} %get-tuple-element.419), channel_id=1, source_target_pairs={{0,1},{1,0},{2,3},{3,2},{4,5},{5,4},{6,7},{7,6},{8,9},{9,8},{10,11... | collective-permute-start | bytes 3538952 | tf_op jit(solution)/shard_map/ppermute | solution.py:677
  89.9 15.7 %collective-permute-start.28 = (bf16[384,768]{1,0:T(8,128)(2,1)S(1)}, bf16[384,768]{1,0:T(8,128)(2,1)S(1)}, u32[]{:S(2)}, u32[]{:S(2)}) collective-permute-start(bf16[384,768]{1,0:T(8,128)(2,1)S(1)} %get-tuple-element.421), channel_id=1, source_target_pairs={{0,4},{4,0},{8,12},{12,8},{16,20},{20,16},{24,28},{28,24},{1,5},{5... | collective-permute-start | bytes 1769480 | tf_op jit(solution)/shard_map/ppermute | solution.py:843
  91.6 15.4 %collective-permute-start.27 = (bf16[384,768]{1,0:T(8,128)(2,1)S(1)}, bf16[384,768]{1,0:T(8,128)(2,1)S(1)}, u32[]{:S(2)}, u32[]{:S(2)}) collective-permute-start(bf16[384,768]{1,0:T(8,128)(2,1)S(1)} %advance.7.refs_1_), channel_id=1, source_target_pairs={{0,8},{4,12},{8,0},{12,4},{16,24},{20,28},{24,16},{28,20},{1,9},{5... | collective-permute-start | bytes 1769480 | tf_op jit(solution)/shard_map/ppermute | solution.py:847
  93.2 14.1 %collective-permute-start.29 = (bf16[256,768]{1,0:T(8,128)(2,1)S(1)}, bf16[256,768]{1,0:T(8,128)(2,1)S(1)}, u32[]{:S(2)}, u32[]{:S(2)}) collective-permute-start(bf16[256,768]{1,0:T(8,128)(2,1)S(1)} %get-tuple-element.426.refs_2_), channel_id=1, source_target_pairs={{0,2},{1,3},{2,0},{3,1},{4,6},{5,7},{6,4},{7,5},{8,10},{9,11},{10,... | collective-permute-start | bytes 1179656 | tf_op jit(solution)/shard_map/ppermute | solution.py:677
  107.8 15.7 %collective-permute-start.32 = (bf16[384,768]{1,0:T(8,128)(2,1)S(1)}, bf16[384,768]{1,0:T(8,128)(2,1)S(1)}, u32[]{:S(2)}, u32[]{:S(2)}) collective-permute-start(bf16[384,768]{1,0:T(8,128)(2,1)S(1)} %get-tuple-element.437), channel_id=1, source_target_pairs={{0,4},{4,0},{8,12},{12,8},{16,20},{20,16},{24,28},{28,24},{1,5},{5... | collective-permute-start | bytes 1769480 | tf_op jit(solution)/shard_map/ppermute | solution.py:843
  108.3 15.4 %collective-permute-start.31 = (bf16[384,768]{1,0:T(8,128)(2,1)S(1)}, bf16[384,768]{1,0:T(8,128)(2,1)S(1)}, u32[]{:S(2)}, u32[]{:S(2)}) collective-permute-start(bf16[384,768]{1,0:T(8,128)(2,1)S(1)} %get-tuple-element.435.refs_1_), channel_id=1, source_target_pairs={{0,8},{4,12},{8,0},{12,4},{16,24},{20,28},{24,16},{28,20},{1,9},{5... | collective-permute-start | bytes 1769480 | tf_op jit(solution)/shard_map/ppermute | solution.py:847
  110.0 13.7 %collective-permute-start.30 = (bf16[384,768]{1,0:T(8,128)(2,1)S(1)}, bf16[384,768]{1,0:T(8,128)(2,1)S(1)}, u32[]{:S(2)}, u32[]{:S(2)}) collective-permute-start(bf16[384,768]{1,0:T(8,128)(2,1)S(1)} %get-tuple-element.436.refs_2_), channel_id=1, source_target_pairs={{8,16},{12,20},{16,8},{20,12},{9,17},{13,21},{17,9},{21,13},{10,18... | collective-permute-start | bytes 1769480 | tf_op jit(solution)/shard_map/ppermute | solution.py:849
  110.9 20.5 %collective-permute-start.37 = (bf16[512,768]{1,0:T(8,128)(2,1)S(1)}, bf16[512,768]{1,0:T(8,128)(2,1)S(1)}, u32[]{:S(2)}, u32[]{:S(2)}) collective-permute-start(bf16[512,768]{1,0:T(8,128)(2,1)S(1)} %add_convert_fusion.refs_1_), channel_id=1, source_target_pairs={{0,2},{1,3},{2,0},{3,1},{4,6},{5,7},{6,4},{7,5},{8,10},{9,11},{10,... | collective-permute-start | bytes 2359304 | tf_op jit(solution)/shard_map/ppermute | solution.py:677
  124.1 14.8 %collective-permute-start.36 = (bf16[384,768]{1,0:T(8,128)(2,1)S(1)}, bf16[384,768]{1,0:T(8,128)(2,1)S(1)}, u32[]{:S(2)}, u32[]{:S(2)}) collective-permute-start(bf16[384,768]{1,0:T(8,128)(2,1)S(1)} %get-tuple-element.466), channel_id=1, source_target_pairs={{0,4},{4,0},{8,12},{12,8},{16,20},{20,16},{24,28},{28,24},{1,5},{5... | collective-permute-start | bytes 1769480 | tf_op jit(solution)/shard_map/ppermute | solution.py:843
  125.7 17.3 %collective-permute-start.35 = (bf16[384,768]{1,0:T(8,128)(2,1)S(1)}, bf16[384,768]{1,0:T(8,128)(2,1)S(1)}, u32[]{:S(2)}, u32[]{:S(2)}) collective-permute-start(bf16[384,768]{1,0:T(8,128)(2,1)S(1)} %get-tuple-element.465), channel_id=1, source_target_pairs={{0,8},{4,12},{8,0},{12,4},{16,24},{20,28},{24,16},{28,20},{1,9},{5... | collective-permute-start | bytes 1769480 | tf_op jit(solution)/shard_map/ppermute | solution.py:847
  130.5 12.5 %collective-permute-start.34 = (bf16[384,768]{1,0:T(8,128)(2,1)S(1)}, bf16[384,768]{1,0:T(8,128)(2,1)S(1)}, u32[]{:S(2)}, u32[]{:S(2)}) collective-permute-start(bf16[384,768]{1,0:T(8,128)(2,1)S(1)} %get-tuple-element.463.refs_2_), channel_id=1, source_target_pairs={{8,16},{12,20},{16,8},{20,12},{9,17},{13,21},{17,9},{21,13},{10,18... | collective-permute-start | bytes 1769480 | tf_op jit(solution)/shard_map/ppermute | solution.py:849
  143.6 13.7 %collective-permute-start.40 = (bf16[384,768]{1,0:T(8,128)(2,1)S(1)}, bf16[384,768]{1,0:T(8,128)(2,1)S(1)}, u32[]{:S(2)}, u32[]{:S(2)}) collective-permute-start(bf16[384,768]{1,0:T(8,128)(2,1)S(1)} %get-tuple-element.508.refs_0_), channel_id=1, source_target_pairs={{0,4},{4,0},{8,12},{12,8},{16,20},{20,16},{24,28},{28,24},{1,5},{5... | collective-permute-start | bytes 1769480 | tf_op jit(solution)/shard_map/ppermute | solution.py:845
  144.1 15.2 %collective-permute-start.39 = (bf16[384,768]{1,0:T(8,128)(2,1)S(1)}, bf16[384,768]{1,0:T(8,128)(2,1)S(1)}, u32[]{:S(2)}, u32[]{:S(2)}) collective-permute-start(bf16[384,768]{1,0:T(8,128)(2,1)S(1)} %get-tuple-element.507), channel_id=1, source_target_pairs={{0,8},{4,12},{8,0},{12,4},{16,24},{20,28},{24,16},{28,20},{1,9},{5... | collective-permute-start | bytes 1769480 | tf_op jit(solution)/shard_map/ppermute | solution.py:847
  159.5 13.4 %collective-permute-start.45 = (bf16[384,768]{1,0:T(8,128)(2,1)S(1)}, bf16[384,768]{1,0:T(8,128)(2,1)S(1)}, u32[]{:S(2)}, u32[]{:S(2)}) collective-permute-start(bf16[384,768]{1,0:T(8,128)(2,1)S(1)} %get-tuple-element.527.refs_0_), channel_id=1, source_target_pairs={{0,4},{4,0},{8,12},{12,8},{16,20},{20,16},{24,28},{28,24},{1,5},{5... | collective-permute-start | bytes 1769480 | tf_op jit(solution)/shard_map/ppermute | solution.py:845
  161.1 14.0 %collective-permute-start.44 = (bf16[384,768]{1,0:T(8,128)(2,1)S(1)}, bf16[384,768]{1,0:T(8,128)(2,1)S(1)}, u32[]{:S(2)}, u32[]{:S(2)}) collective-permute-start(bf16[384,768]{1,0:T(8,128)(2,1)S(1)} %get-tuple-element.526.refs_1_), channel_id=1, source_target_pairs={{0,8},{4,12},{8,0},{12,4},{16,24},{20,28},{24,16},{28,20},{1,9},{5... | collective-permute-start | bytes 1769480 | tf_op jit(solution)/shard_map/ppermute | solution.py:847
  175.3 16.8 %collective-permute-start.49 = (bf16[384,768]{1,0:T(8,128)(2,1)S(1)}, bf16[384,768]{1,0:T(8,128)(2,1)S(1)}, u32[]{:S(2)}, u32[]{:S(2)}) collective-permute-start(bf16[384,768]{1,0:T(8,128)(2,1)S(1)} %get-tuple-element.546.refs_0_), channel_id=1, source_target_pairs={{0,4},{4,0},{8,12},{12,8},{16,20},{20,16},{24,28},{28,24},{1,5},{5... | collective-permute-start | bytes 1769480 | tf_op jit(solution)/shard_map/ppermute | solution.py:845
  175.9 16.2 %collective-permute-start.48 = (bf16[384,768]{1,0:T(8,128)(2,1)S(1)}, bf16[384,768]{1,0:T(8,128)(2,1)S(1)}, u32[]{:S(2)}, u32[]{:S(2)}) collective-permute-start(bf16[384,768]{1,0:T(8,128)(2,1)S(1)} %get-tuple-element.545.refs_0_), channel_id=1, source_target_pairs={{0,8},{4,12},{8,0},{12,4},{16,24},{20,28},{24,16},{28,20},{1,9},{5... | collective-permute-start | bytes 1769480 | tf_op jit(solution)/shard_map/ppermute | solution.py:847
  179.6 12.5 %collective-permute-start.50 = (f32[8,2496]{1,0:T(8,128)S(1)}, f32[8,2496]{1,0:T(8,128)S(1)}, u32[]{:S(2)}, u32[]{:S(2)}) collective-permute-start(f32[8,2496]{1,0:T(8,128)S(1)} %pad_maximum_fusion.5), channel_id=1, source_target_pairs={{0,8},{4,12},{8,0},{12,4},{16,24},{20,28},{24,16},{28,20},{1,9},{5... | collective-permute-start | bytes 239624 | tf_op jit(solution)/shard_map/ppermute | solution.py:686
  179.6 12.5 %collective-permute-start.51 = (bf16[256,768]{1,0:T(8,128)(2,1)S(1)}, bf16[256,768]{1,0:T(8,128)(2,1)S(1)}, u32[]{:S(2)}, u32[]{:S(2)}) collective-permute-start(bf16[256,768]{1,0:T(8,128)(2,1)S(1)} %get-tuple-element.550.refs_0_), channel_id=1, source_target_pairs={{0,1},{1,0},{2,3},{3,2},{4,5},{5,4},{6,7},{7,6},{8,9},{9,8},{10,11... | collective-permute-start | bytes 1179656 | tf_op jit(solution)/shard_map/ppermute | solution.py:677
  179.6 12.5 %collective-permute-start.52 = (bf16[256,768]{1,0:T(8,128)(2,1)S(1)}, bf16[256,768]{1,0:T(8,128)(2,1)S(1)}, u32[]{:S(2)}, u32[]{:S(2)}) collective-permute-start(bf16[256,768]{1,0:T(8,128)(2,1)S(1)} %get-tuple-element.551.refs_1_), channel_id=1, source_target_pairs={{0,1},{1,0},{2,3},{3,2},{4,5},{5,4},{6,7},{7,6},{8,9},{9,8},{10,11... | collective-permute-start | bytes 1179656 | tf_op jit(solution)/shard_map/ppermute | solution.py:677
  (52 other events, 330.4 us)
